TPU v7x, 128 devices: a whole 4x4x4 slice. The times are simulated.
128 devices in a mesh: seq: 16 (over z_hi, x, core), chan: 8 (over z_lo, y).
Axes of the slice: x: 4, y: 4, z: 4 (z_hi: 2, z_lo: 2; z = z_hi * 2 + z_lo), core: 2. Of those that a mesh axis runs over, the one named last changes fastest.
Arguments:
- tokens: bfloat16 [4096, 8192], P('seq', 'chan'), may hold values from -6 to 6
- input_weight: bfloat16 [3, 8192, 8192], P(None, 'seq', 'chan'), may hold values from -0.0625 to 0.0625
- filter_taps: float32 [128, 8192], P(None, 'chan'), may hold values from -0.9 to 0.9
- decay_rates: float32 [8192], P('chan'), may hold values from 0.003 to 0.3
- skip_gain: float32 [8192], P('chan'), may hold values from 0.5 to 1.5
- owners: int32 [512, 1], P('seq'), may hold values from 0 to 15; in each aligned block of 32 rows (0 to 31, 32 to 63, ...) at most 2 rows name the same one
Outputs:
- gated: bfloat16 [4096, 8192], P('seq', 'chan')
- handed: bfloat16 [512, 8, 8192], P('seq', None, 'chan')
Inputs may be any that keep to these rules, and one draw needn't show every extreme that they name: Among the 32 pages of one device each of the 16 owners is named exactly 2 times, so every row of handed is filled.
All inputs are finite; a program needn't handle non-finite values.
Results may differ from a plain program's by a relative error of at most 0.018.
Values may be sent and summed in bfloat16 or wider, within the bound.
A program may use at most 128 MiB of HBM per device.

v0:
```python
import jax
import jax.numpy as jnp
from jax import lax
from jax.sharding import PartitionSpec as P

PAGE_ROWS = 8
CAP = 2


def shifted_2(value, axis, steps):
    count = lax.axis_size(axis)
    leading, last = (max(0, -steps), min(count, count - steps))
    return lax.ppermute(value, axis, [(source, source + steps) for source in range(leading, last)])


def handoff_page_list(u_values, owners):
    owner_count = lax.axis_size("seq")
    rows_per_page = u_values.reshape(u_values.shape[0] // PAGE_ROWS, PAGE_ROWS, u_values.shape[1])
    owner = owners[:, 0]
    onehot = (owner[:, None] == jnp.arange(owner_count, dtype=jnp.int32)[None, :]).astype(jnp.int32)
    earlier = jnp.cumsum(onehot, axis=0) - onehot
    slot = jnp.sum(earlier * onehot, axis=1)
    target = owner * CAP + slot
    select = (target[None, :] == jnp.arange(owner_count * CAP, dtype=jnp.int32)[:, None]).astype(
        jnp.bfloat16
    )
    buffer = jnp.einsum(
        "sp,prk->srk", select, rows_per_page, preferred_element_type=jnp.float32
    ).astype(jnp.bfloat16)
    return lax.all_to_all(buffer, "seq", split_axis=0, concat_axis=0, tiled=True)


def lag_filter(extended, taps, rows):
    taps_count = taps.shape[0]

    def add_group(group, total):
        for inner in range(8):
            lag = group * 8 + inner
            shifted = lax.dynamic_slice_in_dim(extended, taps_count - 1 - lag, rows, 0)
            weight_row = lax.dynamic_slice_in_dim(taps, lag, 1, 0)
            total = total + weight_row * shifted
        return total

    return lax.fori_loop(
        0, taps_count // 8, add_group, jnp.zeros((rows, extended.shape[1]), jnp.float32)
    )


def per_device(tokens, input_weight, filter_taps, decay_rates, skip_gain, owners):
    whole = lax.all_gather(tokens, "chan", axis=1, tiled=True)
    rows_here = whole.shape[0]
    rows_grouped = lax.all_to_all(whole, "seq", split_axis=1, concat_axis=0, tiled=True)
    summed = lax.psum_scatter(
        jnp.einsum("xy,iyz->xiz", rows_grouped, input_weight, preferred_element_type=jnp.float32),
        "seq",
        scatter_dimension=0,
        tiled=True,
    )
    query = summed[:, 0, :].astype(jnp.bfloat16)
    key_part = summed[:, 1, :].astype(jnp.bfloat16)
    value_slice = summed[:, 2, :].astype(jnp.bfloat16)
    u_values = (key_part.astype(jnp.float32) * value_slice.astype(jnp.float32)).astype(jnp.bfloat16)
    taps_count = filter_taps.shape[0]
    earlier_rows = shifted_2(u_values[rows_here - (taps_count - 1) :], "seq", 1)
    extended = jnp.concatenate([earlier_rows, u_values], axis=0).astype(jnp.float32)
    lags = jnp.arange(taps_count, dtype=jnp.float32)
    taps = filter_taps * jnp.exp(-decay_rates[None, :] * lags[:, None])
    filter_response = lag_filter(extended, taps, rows_here)
    u_float = u_values.astype(jnp.float32)
    mixed = filter_response + skip_gain[None, :] * u_float
    gated = (query.astype(jnp.float32) * mixed).astype(jnp.bfloat16)
    handed = handoff_page_list(u_values, owners)
    return (gated, handed)


def solution(mesh):
    return jax.shard_map(
        per_device,
        mesh=mesh,
        in_specs=(
            P("seq", "chan"),
            P(None, "seq", "chan"),
            P(None, "chan"),
            P("chan"),
            P("chan"),
            P("seq", None),
        ),
        out_specs=(P("seq", "chan"), P("seq", None, "chan")),
        check_vma=False,
    )
```

profile of v0, /device:TPU:0, one launch (start us, length us, event | category | flops | bytes accessed | tf_op | source)
XLA Modules:
  0.0 558.7 jit_solution(8695423867414020234)
XLA Ops:
  7.2 0.0 copy-start
  7.2 0.0 all-gather.2.cloned.1.call-start
  7.2 0.7 all-gather.2.cloned.1.call-update
  7.9 0.0 reduce-scatter.2.cloned.1.call-start
  8.0 56.9 %all-gather.2.cloned.1.call-done = bf16[256,8192]{1,0:T(8,128)(2,1)} async-done(((bf16[256,1024]{1,0:T(8,128)(2,1)}), bf16[256,8192]{1,0:T(8,128)(2,1)}) %all-gather.2.cloned.1.call-update) | async-done | bytes 4194320 | tf_op jit(solution)/shard_map/all_gather | solution.py:50
  64.8 2.6 copy.18
  67.5 58.2 %all_to_all.24 = bf16[256,16,512]{2,0,1:T(8,128)(2,1)} all-to-all(bf16[256,16,512]{2,0,1:T(8,128)(2,1)S(1)} %bitcast.52), channel_id=1, replica_groups=mesh['seq'=16,'chan'=8] {'seq'}, dimensions={1} | all-to-all | bytes 8388608 | tf_op jit(solution)/shard_map/all_to_all | solution.py:52
  125.7 0.0 copy-done
  125.7 22.7 %fusion.14 = f32[4096,3,1024]{2,0,1:T(8,128)} fusion(bf16[4096,512,1]{1,0,2:T(8,128)(2,1)} %bitcast.54, bf16[3,512,1024]{2,1,0:T(8,128)(2,1)S(1)} %copy-done), kind=kOutput, calls=%fused_computation.36 | convolution fusion | flops 12884901888 | bytes 57671680 | tf_op jit(solution)/shard_map/xy,iyz->xiz/dot_general | solution.py:54
  148.4 0.0 copy-start.4
  148.4 0.0 copy-start.5
  148.4 0.0 copy-start.2
  148.4 0.0 reduce-scatter.2.cloned.1.call-update
  148.5 0.6 copy-done.4
  149.1 0.0 copy-done.5
  149.1 0.1 fusion.10
  149.2 0.1 reduce_window_sum.11
  149.3 0.2 select_reduce_fusion
  149.5 0.1 copy-done.2
  149.5 0.1 exponential_multiply_fusion
  149.6 323.1 %reduce-scatter.2.cloned.1.call-done = f32[256,3,1024]{2,0,1:T(8,128)} async-done(((f32[4096,3,1024]{2,0,1:T(8,128)}), f32[256,3,1024]{2,0,1:T(8,128)}) %reduce-scatter.2.cloned.1.call-update) | async-done | bytes 3145744 | tf_op jit(solution)/shard_map/reduce_scatter | solution.py:53
  472.7 1.7 multiply_convert_fusion
  474.4 0.1 slice_bitcast_fusion
  474.5 1.3 collective-permute-start
  475.8 1.7 fusion.17
  477.5 0.8 convolution_convert_fusion
  478.2 1.1 copy.13
  479.3 6.9 %all-to-all-start.1 = ((bf16[32,8,1024]{2,1,0:T(8,128)(2,1)}), bf16[32,8,1024]{2,1,0:T(8,128)(2,1)}, u32[]{:S(2)}, u32[]{:S(2)}) async-start(bf16[32,8,1024]{2,1,0:T(8,128)(2,1)} %copy.13), calls=%async_computation.2 | async-start | bytes 1048576 | tf_op jit(solution)/shard_map/all_to_all | solution.py:30
  486.2 1.7 fusion.18
  487.9 0.0 collective-permute-done
  487.9 0.2 maximum_convert_fusion
  488.1 0.0 copy-start.3
  488.1 58.4 %while.17 = (s32[]{:T(128)}, f32[256,1024]{1,0:T(8,128)}, f32[128,1024]{1,0:T(8,128)S(1)}, f32[383,1024]{1,0:T(8,128)S(1)}, s32[]{:T(128)}, /*index=5*/s32[]{:T(...) while((s32[]{:T(128)}, f32[256,1024]{1,0:T(8,128)}, ...), condition=%wide.region_2.0_spmd.clone, body=%wide.region_1.0_spmd.clone.sunk | while | flops 4456515 | bytes 10585079 | solution.py:44
  488.3 2.4 fusion.20
  490.8 3.6 fusion.20
  494.5 3.6 fusion.20
  498.2 3.6 fusion.20
  501.9 3.6 fusion.20
  505.6 3.6 fusion.20
  509.4 3.6 fusion.20
  513.1 3.6 fusion.20
  516.8 3.6 fusion.20
  520.5 3.6 fusion.20
  524.2 3.6 fusion.20
  528.0 3.6 fusion.20
  531.7 3.6 fusion.20
  535.4 3.6 fusion.20
  539.1 3.6 fusion.20
  542.8 3.6 fusion.20
  546.5 0.0 copy-start.1
  546.5 0.0 copy-done.3
  546.5 3.6 fusion.7
  550.0 0.0 all-to-all-done.1
  550.0 1.9 copy.26
  551.9 0.0 copy-done.1
  (19 shorter events, 0.6 us)
Async XLA Ops:
  7.2 118.6 %copy-start = (bf16[3,512,1024]{2,1,0:T(8,128)(2,1)S(1)}, bf16[3,512,1024]{2,1,0:T(8,128)(2,1)}, u32[]{:S(2)}) copy-start(bf16[3,512,1024]{2,1,0:T(8,128)(2,1)} %param.9) | copy-start | bytes 9437188
  7.2 57.7 %all-gather.2.cloned.1.call-start = ((), (), s32[]{:S(2)}) async-start(), calls=%async_computation.3 | async-start | bytes 4718592 | tf_op jit(solution)/shard_map/all_gather | solution.py:50
  7.9 464.8 %reduce-scatter.2.cloned.1.call-start = ((), (), s32[]{:S(2)}) async-start(), calls=%async_computation.4 | async-start | bytes 53477376 | tf_op jit(solution)/shard_map/reduce_scatter | solution.py:53
  148.4 0.7 copy-start.4
  148.4 0.7 copy-start.5
  148.4 1.1 copy-start.2
  474.5 13.4 %collective-permute-start = (bf16[127,1024]{1,0:T(8,128)(2,1)S(1)}, bf16[127,1024]{1,0:T(8,128)(2,1)S(1)}, u32[]{:S(2)}, u32[]{:S(2)}) collective-permute-start(bf16[127,1024]{1,0:T(8,128)(2,1)S(1)} %slice_bitcast_fusion), channel_id=1, source_target_pairs={{0,8},{8,16},{16,24},{24,32},{32,40},{40,48},{48,56},{56,64},{64,7... | collective-permute-start | bytes 780296 | tf_op jit(solution)/shard_map/ppermute | solution.py:13
  479.3 70.7 %all-to-all-start.1 = ((bf16[32,8,1024]{2,1,0:T(8,128)(2,1)}), bf16[32,8,1024]{2,1,0:T(8,128)(2,1)}, u32[]{:S(2)}, u32[]{:S(2)}) async-start(bf16[32,8,1024]{2,1,0:T(8,128)(2,1)} %copy.13), calls=%async_computation.2 | async-start | bytes 1048576 | tf_op jit(solution)/shard_map/all_to_all | solution.py:30
  488.1 58.4 %copy-start.3 = (f32[1024]{0:T(1024)S(1)}, f32[1024]{0:T(1024)}, u32[]{:S(2)}) copy-start(f32[1024]{0:T(1024)} %param.12) | copy-start | bytes 12292
  546.5 5.4 copy-start.1
Sparse Core Ops, SparseCore 0:
  9.7 55.1 all-gather.1
  148.6 324.0 reduce-scatter.1
where the time goes:
time: 561 us; the launch traced here: 559 us
  waiting for transfers between devices  381 us (68%)
  other arithmetic  65.8 us (12%)
  blocking collectives  58.2 us (10%)
  matrix products  23.5 us (4%)
  between operations  14.2 us (3%)
  starting transfers between devices  8.25 us (1%)
  local copies, waits for them, and re-layouts  6.93 us (1%)
    reduce_scatter x1, waiting for transfers between devices, per_device(): lax.psum_scatter(jnp.einsum('xy,iyz->xiz', rows_grouped, input_weight, pr...  323 us
    all_to_all x1, blocking collectives, per_device(): lax.all_to_all(whole, 'seq', split_axis=1, concat_axis=0, tiled=True)  58.2 us
    all_gather x1, waiting for transfers between devices, per_device(): whole = lax.all_gather(tokens, 'chan', axis=1, tiled=True)  56.9 us
    add x16, other arithmetic, add_group(): total = total + weight_row * shifted  56.6 us
    dot_general x1, matrix products, per_device(): jnp.einsum('xy,iyz->xiz', rows_grouped, input_weight, preferred_element_t...  22.7 us
  transfers between devices with their start and end apart: 4, of which 2 were waited for; matrix products, arithmetic and copies ran while one was open for 12% of the time, Pallas kernels for 0%

commit v1 on v0

v1 whole, which is shorter than its diff:
```python
import jax
import jax.numpy as jnp
from jax import lax
from jax.experimental import pallas as pl
from jax.experimental.pallas import tpu as pltpu
from jax.sharding import PartitionSpec as P

MESH = pl.DeviceIdType.MESH
F32, BF16 = jnp.float32, jnp.bfloat16
CHUNKS, LANES = 8, 128
ROWS, HALF = 256, 512
WINDOW = 3


def kernel(tok, wgt, taps_in, decay, skip, owners, gated, handed,
           wbuf, tbuf, own, osend, orecv, qbuf, ubuf, hrecv, psend, pbuf, sel, taps, shifts,
           wl, ws, wr, tzs, tzr, tys, tyr, os_, or_, hs, hr, ps, pr):
    s, c = lax.axis_index("seq"), lax.axis_index("chan")
    core, x, zh = s % 2, (s // 2) % 4, s // 8
    zl, y = c // 4, c % 4

    def dev(zh_, x_, core_, zl_, y_):
        return ((zh_ * 4 + x_) * 2 + core_, zl_ * 4 + y_)

    def remote(src, dst, ss, rs, to):
        return pltpu.make_async_remote_copy(
            src_ref=src, dst_ref=dst, send_sem=ss, recv_sem=rs, device_id=to, device_id_type=MESH)

    def kb(dx):
        return ((x + dx) % 4) * 2 + core

    def load(j):
        return pltpu.make_async_copy(
            wgt.at[:, :, pl.ds(pl.multiple_of(j * LANES, LANES), LANES)], wbuf.at[j, kb(0)], wl.at[j])

    @pl.loop(0, CHUNKS)
    def _(j):
        load(j).start()

    barrier = pltpu.get_barrier_semaphore()

    @pl.loop(1, 16)
    def _(o):
        pl.semaphore_signal(barrier, inc=1, device_id=((s + o) % 16, c), device_id_type=MESH)

    for dy in (1, 2, 3):
        pl.semaphore_signal(barrier, inc=1, device_id=dev(zh, x, core, zl, (y + dy) % 4), device_id_type=MESH)
    for z in (0, 1):
        pl.semaphore_signal(barrier, inc=1, device_id=dev(z, x, core, 1 - zl, y), device_id_type=MESH)
    pl.semaphore_wait(barrier, 20)

    def w_plus(j):
        return remote(wbuf.at[j, kb(0)], wbuf.at[j, kb(0)], ws.at[0, j], wr.at[0, j], dev(zh, (x + 1) % 4, core, zl, y))

    def w_minus(j):
        return remote(wbuf.at[j, kb(0)], wbuf.at[j, kb(0)], ws.at[1, j], wr.at[1, j], dev(zh, (x + 3) % 4, core, zl, y))

    def w_far(j):
        way = 1 + 2 * (j % 2)
        block = wbuf.at[j, ((x + 4 - way) % 4) * 2 + core]
        return remote(block, block, ws.at[2, j], wr.at[2, j], dev(zh, (x + way) % 4, core, zl, y))

    def w_pair(j, q):
        block = wbuf.at[j, ((x + q) % 4) * 2 + core]
        return remote(block, block, ws.at[3 + q, j], wr.at[3 + q, j], dev(zh, x, 1 - core, zl, y))

    def w_send(j):
        load(j).wait()
        w_plus(j).start()
        w_minus(j).start()
        w_pair(j, 0).start()

    def t_z(d):
        return remote(tok, tbuf.at[y, zh], tzs.at[d], tzr.at[zh], dev(zl, x, core, d, y))

    def t_own():
        return pltpu.make_async_copy(tok, tbuf.at[y, zh], tzr.at[zh])

    for d in (0, 1):
        stays = jnp.logical_and(zl == zh, zl == d)

        @pl.when(stays)
        def _():
            t_own().start()

        @pl.when(jnp.logical_not(stays))
        def _():
            t_z(d).start()

    @pl.loop(0, WINDOW)
    def _(j):
        w_send(j)

    def t_y(r, dy):
        return remote(tbuf.at[y, r], tbuf.at[y, r], tys.at[r, dy - 1], tyr.at[r, dy - 1],
                      dev(zh, x, core, zl, (y + dy) % 4))

    lag = lax.broadcasted_iota(jnp.int32, (128, LANES), 0)
    for j in range(CHUNKS):
        cols = slice(j * LANES, (j + 1) * LANES)
        value = taps_in[:, cols] * jnp.exp(-decay[:, cols] * lag.astype(F32))
        taps[j] = value + jnp.where(lag == 0, skip[:, cols], 0.0)
    iota = lambda shape, axis: lax.broadcasted_iota(jnp.int32, shape, axis)
    dot = lambda a, b, dims: lax.dot_general(a, b, (dims, ((), ())), preferred_element_type=F32)
    names = jnp.broadcast_to(owners[...], (32, 128))
    onehot = (names == iota((32, 128), 1)).astype(F32)
    before = (iota((32, 32), 1) < iota((32, 32), 0)).astype(BF16)
    earlier = dot(before, onehot.astype(BF16), ((1,), (0,)))
    slot = jnp.sum(earlier * onehot, axis=1, keepdims=True)
    target = owners[...].astype(F32) * 2.0 + slot
    place = (jnp.broadcast_to(target, (32, 32)) == iota((32, 32), 1).astype(F32)).astype(BF16)
    spread = (iota((ROWS, 32), 0) // 8 == iota((ROWS, 32), 1)).astype(BF16)
    part = dot(spread, place, ((1,), (1,))).astype(BF16)
    whole = dot(part, spread, ((1,), (1,)))
    same = (iota((ROWS, ROWS), 0) % 8 == iota((ROWS, ROWS), 1) % 8).astype(F32)
    sel[...] = (whole * same).astype(BF16)

    for r in (0, 1):
        pltpu.make_async_copy(tbuf.at[y, r], tbuf.at[y, r], tzr.at[r]).wait()
        for dy in (1, 3, 2):
            t_y(r, dy).start()

    def o_copy(j):
        return remote(osend.at[j], orecv.at[j], os_.at[j], or_.at[j], dev(1 - zh, x, core, zl, y))

    def h_copy(j):
        after = (s + 1) % 16
        return remote(ubuf.at[j, pl.ds(128, 128)], hrecv.at[j], hs.at[j], hr.at[j], (after, c))

    def p_copy(j, o):
        to = (s + o) % 16
        return remote(psend.at[j, pl.ds(pl.multiple_of(to * 16, 16), 16)],
                      pbuf.at[j, pl.ds(pl.multiple_of(s * 16, 16), 16)], ps.at[j], pr.at[j], (to, c))

    def matmul(j, row):
        def add(xx, total):
            for half in (0, 1):
                w = jnp.concatenate([wbuf[j, xx * 2 + half, p] for p in range(3)], axis=1)
                total = total + jnp.dot(tbuf[xx, row, :, half * HALF:(half + 1) * HALF], w,
                                        preferred_element_type=F32)
            return total
        return lax.fori_loop(0, 4, add, jnp.zeros((ROWS, 3 * LANES), F32))

    def stage_mm(j):
        for q in range(4):
            w_pair(j, q).wait_recv()
        osend[j] = matmul(j, 1 - zh).astype(BF16)
        o_copy(j).start()
        own[j % 2] = matmul(j, zh)

    def stage_u(j):
        o_copy(j).wait_recv()
        full = (own[j % 2] + orecv[j].astype(F32)).astype(BF16)
        qbuf[j] = full[:, :LANES]
        u = (full[:, LANES:2 * LANES].astype(F32) * full[:, 2 * LANES:].astype(F32)).astype(BF16)
        ubuf[j] = u
        h_copy(j).start()
        psend[j] = jnp.dot(sel[...], u, preferred_element_type=F32).astype(BF16)

        @pl.loop(1, 16)
        def _(o):
            p_copy(j, o).start()

        mine = pl.ds(pl.multiple_of(s * 16, 16), 16)
        handed[mine, pl.ds(pl.multiple_of(j * LANES, LANES), LANES)] = psend[j, mine]

    def stage_filter(j):
        h_copy(j).wait_recv()
        u = ubuf[j].astype(F32)
        prior = jnp.where(s == 0, 0.0, hrecv[j].astype(F32))
        ext = jnp.concatenate([prior, u], axis=0)
        for b in range(8):
            shifts[b] = ext[8 - b:384 - b]

        def add(a, total):
            rows = taps[j, pl.ds(pl.multiple_of(a * 8, 8), 8)]
            at = pl.multiple_of(120 - a * 8, 8)
            for b in range(8):
                total = total + rows[b:b + 1] * shifts[b, pl.ds(at, ROWS)]
            return total

        z = lax.fori_loop(0, 16, add, jnp.zeros((ROWS, LANES), F32))
        gated[:, pl.ds(pl.multiple_of(j * LANES, LANES), LANES)] = (qbuf[j].astype(F32) * z).astype(BF16)

    def tick(t):
        @pl.when(t < CHUNKS)
        def _():
            stage_mm(t)

        @pl.when(jnp.logical_and(t >= 1, t <= CHUNKS))
        def _():
            stage_u(t - 1)

        @pl.when(t >= 2)
        def _():
            stage_filter(t - 2)

    def reached(i):
        return jnp.where(i < 5, 0, jnp.where(i >= 8, 10, (i - 4) * 2))

    @pl.loop(0, CHUNKS + 1)
    def _(i):
        @pl.when(i + WINDOW < CHUNKS)
        def _():
            w_send(i + WINDOW)

        @pl.when(i < CHUNKS)
        def _():
            w_plus(i).wait_recv()
            w_minus(i).wait_recv()
            w_far(i).start()
            w_pair(i, 1).start()
            w_pair(i, 3).start()

        @pl.when(i >= 1)
        def _():
            w_far(i - 1).wait_recv()
            w_pair(i - 1, 2).start()

        @pl.when(i == 5)
        def _():
            for r in (0, 1):
                for dy in (1, 3, 2):
                    t_y(r, dy).wait_recv()

        @pl.loop(reached(i - 1), reached(i))
        def _(t):
            tick(t)

    @pl.loop(0, CHUNKS)
    def _(j):
        some = pbuf.at[j, pl.ds(0, 240)]
        pltpu.make_async_copy(some, some, pr.at[j]).wait()
        pltpu.make_async_copy(some, some, ps.at[j]).wait()

        @pl.loop(1, 16)
        def _(o):
            rows = pl.ds(pl.multiple_of(((s + o) % 16) * 16, 16), 16)
            handed[rows, pl.ds(pl.multiple_of(j * LANES, LANES), LANES)] = pbuf[j, rows]

        w_plus(j).wait_send()
        w_minus(j).wait_send()
        w_far(j).wait_send()
        for q in range(4):
            w_pair(j, q).wait_send()
        o_copy(j).wait_send()
        h_copy(j).wait_send()

    for r in (0, 1):
        for dy in (1, 2, 3):
            t_y(r, dy).wait_send()
    for d in (0, 1):
        @pl.when(jnp.logical_not(jnp.logical_and(zl == zh, zl == d)))
        def _():
            t_z(d).wait_send()


def per_device(tokens, input_weight, filter_taps, decay_rates, skip_gain, owners):
    dma = pltpu.SemaphoreType.DMA
    vmem, any_ = pl.BlockSpec(memory_space=pltpu.VMEM), pl.BlockSpec(memory_space=pl.ANY)
    gated, handed = pl.pallas_call(
        kernel,
        out_shape=(jax.ShapeDtypeStruct((ROWS, 1024), BF16), jax.ShapeDtypeStruct((ROWS, 1024), BF16)),
        in_specs=[any_, any_, vmem, vmem, vmem, vmem],
        out_specs=(vmem, vmem),
        scratch_shapes=[
            pltpu.VMEM((CHUNKS, 8, 3, HALF, LANES), BF16),
            pltpu.VMEM((4, 2, ROWS, 1024), BF16),
            pltpu.VMEM((2, ROWS, 3 * LANES), F32),
            pltpu.VMEM((CHUNKS, ROWS, 3 * LANES), BF16),
            pltpu.VMEM((CHUNKS, ROWS, 3 * LANES), BF16),
            pltpu.VMEM((CHUNKS, ROWS, LANES), BF16),
            pltpu.VMEM((CHUNKS, ROWS, LANES), BF16),
            pltpu.VMEM((CHUNKS, 128, LANES), BF16),
            pltpu.VMEM((CHUNKS, ROWS, LANES), BF16),
            pltpu.VMEM((CHUNKS, ROWS, LANES), BF16),
            pltpu.VMEM((ROWS, ROWS), BF16),
            pltpu.VMEM((CHUNKS, 128, LANES), F32),
            pltpu.VMEM((8, 376, LANES), F32),
            dma((CHUNKS,)), dma((7, CHUNKS)), dma((7, CHUNKS)),
            dma((2,)), dma((2,)), dma((2, 3)), dma((2, 3)),
            dma((CHUNKS,)), dma((CHUNKS,)), dma((CHUNKS,)), dma((CHUNKS,)), dma((CHUNKS,)), dma((CHUNKS,)),
        ],
        compiler_params=pltpu.CompilerParams(
            collective_id=0, has_side_effects=True, vmem_limit_bytes=56 * 1024 * 1024),
        name="hyena",
    )(tokens, input_weight, filter_taps, decay_rates.reshape(1, -1), skip_gain.reshape(1, -1), owners)
    return gated, handed.reshape(32, 8, 1024)


def solution(mesh):
    return jax.shard_map(
        per_device,
        mesh=mesh,
        in_specs=(P("seq", "chan"), P(None, "seq", "chan"), P(None, "chan"), P("chan"), P("chan"), P("seq", None)),
        out_specs=(P("seq", "chan"), P("seq", None, "chan")),
        check_vma=False,
    )
```

time: 561 us -> 167 us (0.30)
  waiting for transfers between devices: 381 us -> 0 us
  Pallas kernels: 0 us -> 161 us
  other arithmetic: 65.8 us -> 0 us
  blocking collectives: 58.2 us -> 0 us
  matrix products: 23.5 us -> 0 us
  between operations: 14.2 us -> 0.64 us
  starting transfers between devices: 8.25 us -> 0 us
    reduce_scatter x1 -> x0, waiting for transfers between devices: 323 us -> none  [per_device(): lax.psum_scatter(jnp.einsum('xy,iyz->xiz', rows_grouped, input_weight, pr...]
    pallas_call x0 -> x1, Pallas kernels: none -> 161 us  [per_device(): pl.pallas_call(kernel, out_shape=(jax.ShapeDtypeStruct((ROWS, 1024), BF16...]
    all_to_all x1 -> x0, blocking collectives: 58.2 us -> none  [per_device(): lax.all_to_all(whole, 'seq', split_axis=1, concat_axis=0, tiled=True)]
    all_gather x1 -> x0, waiting for transfers between devices: 56.9 us -> none  [per_device(): whole = lax.all_gather(tokens, 'chan', axis=1, tiled=True)]
    add x17 -> x0, other arithmetic: 56.6 us -> none  [the longest x16 56.6 us: add_group(): total = total + weight_row * shifted]
    dot_general x2 -> x0, matrix products: 23.5 us -> none  [the longest x1 22.7 us: per_device(): jnp.einsum('xy,iyz->xiz', rows_grouped, input_weight, preferred_element_t...]
    convert_element_type x6 -> x0, other arithmetic: 8.83 us -> none  [the longest x3 5.02 us: per_device(): (key_part.astype(jnp.float32) * value_slice.astype(jnp.float32)).astype(j...]
    all_to_all x1 -> x0, starting transfers between devices: 6.87 us -> none  [handoff_page_list(): lax.all_to_all(buffer, 'seq', split_axis=0, concat_axis=0, tiled=True)]
  transfers between devices with their start and end apart: 4 -> 0, of which waited for: 2 -> 0; matrix products, arithmetic and copies ran while one was open for 12% -> 0% of each run, Pallas kernels for 0% -> 0%
where the time goes in v1:
time: 167 us
  Pallas kernels  161 us (96%)
  local copies, waits for them, and re-layouts  5.08 us (3%)
    pallas_call x1, Pallas kernels, per_device(): pl.pallas_call(kernel, out_shape=(jax.ShapeDtypeStruct((ROWS, 1024), BF16...  161 us
    unnamed x3, local copies, waits for them, and re-layouts  5.08 us

profile of v1, /device:TPU:0, one launch (start us, length us, event | category | flops | bytes accessed | tf_op | source)
XLA Modules:
  0.0 166.5 jit_solution(6287785051704254692)
XLA Ops:
  0.6 1.3 copy.8.owners
  2.0 160.8 %hyena.1 = (bf16[256,1024]{1,0:T(8,128)(2,1)}, bf16[256,1024]{1,0:T(8,128)(2,1)}) custom-call(bf16[256,1024]{1,0:T(8,128)(2,1)} %tok.1, bf16[3,512,1024]{2,1,0:T(8,128)(2,1)} %wgt.1, f32[128,1024]{1,0:T(8,128)} %taps_in.1, f32[1,1024]{1,0:T(1,128)} %bitcast.4, f32[1,1024]{1,0:T(1,128)} %bitcast.5, s32[32,1]{1,0:T(8,128)} %copy.8.owners), custom_call_target="tpu_custom_call" | custom-call | tf_op jit(solution)/shard_map/hyena/pallas_call | solution.py:261
  162.8 1.9 %copy.11 = bf16[256,1024]{1,0:T(8,128)(2,1)} copy(bf16[256,1024]{1,0:T(8,128)(2,1)} %get-tuple-element.8) | data formatting | bytes 1048576
  164.7 1.9 %copy.12 = bf16[32,8,1024]{2,1,0:T(8,128)(2,1)} copy(bf16[32,8,1024]{2,1,0:T(8,128)(2,1)} %bitcast.3) | data formatting | bytes 1048576

commit v2 on v0

v2 whole, which is shorter than its diff:
```python
import jax
import jax.numpy as jnp
from jax import lax
from jax.experimental import pallas as pl
from jax.experimental.pallas import tpu as pltpu
from jax.sharding import PartitionSpec as P

MESH = pl.DeviceIdType.MESH
F32, BF16 = jnp.float32, jnp.bfloat16
CHUNKS, LANES = 4, 128
ROWS, HALF, SUB = 256, 512, 128
MESSAGES = 8


def kernel(tok, wgt, taps_in, decay, skip, owners, gated, handed,
           wbuf, wother, tbuf, txbuf, osend, orecv, qbuf, ubuf, hrecv, psend, pbuf, gsend, grecv,
           mine, theirs, sel, taps, shifts,
           wl, ws, wr, txs, txr, tzs, tzr, tys, tyr, os_, or_, hs, hr, ps, pr, gs, gr, ms, mr):
    s, c = lax.axis_index("seq"), lax.axis_index("chan")
    core, x, zh = s % 2, (s // 2) % 4, s // 8
    zl, y = c // 4, c % 4
    zo, x2 = 1 - zh, (x + 2) % 4

    def dev(zh_, x_, core_, zl_, y_):
        return ((zh_ * 4 + x_) * 2 + core_, zl_ * 4 + y_)

    def remote(src, dst, ss, rs, to):
        return pltpu.make_async_remote_copy(
            src_ref=src, dst_ref=dst, send_sem=ss, recv_sem=rs, device_id=to, device_id_type=MESH)

    def at(start, size):
        return pl.ds(pl.multiple_of(start * size, size), size)

    def group(j):
        return ((x + j % 2) // 2) % 2

    def beside(j):
        up = 1 - 2 * ((x + j) % 2)
        return (x + 4 + up) % 4

    def across(j):
        up = 1 - 2 * ((x + j + 1) % 2)
        return (x + 4 + up) % 4

    def kb(xx):
        return xx * 2 + core

    def load(j):
        return pltpu.make_async_copy(wgt.at[:, :, at(2 * j + group(j), LANES)], wbuf.at[j, kb(x)], wl.at[0, j])

    def load_other(j):
        return pltpu.make_async_copy(wgt.at[:, :, at(2 * j + 1 - group(j), LANES)], wother.at[j], wl.at[1, j])

    @pl.loop(0, CHUNKS)
    def _(j):
        load(j).start()
        load_other(j).start()

    barrier = pltpu.get_barrier_semaphore()

    @pl.loop(1, 16)
    def _(o):
        pl.semaphore_signal(barrier, inc=1, device_id=((s + o) % 16, c), device_id_type=MESH)

    for dy in (1, 2, 3):
        pl.semaphore_signal(barrier, inc=1, device_id=dev(zh, x, core, zl, (y + dy) % 4), device_id_type=MESH)
    for z in (0, 1):
        pl.semaphore_signal(barrier, inc=1, device_id=dev(z, x, core, 1 - zl, y), device_id_type=MESH)
    pl.semaphore_wait(barrier, 20)

    def w_beside(j):
        return remote(wbuf.at[j, kb(x)], wbuf.at[j, kb(x)], ws.at[0, j], wr.at[0, j], dev(zh, beside(j), core, zl, y))

    def w_across(j):
        return remote(wother.at[j], wbuf.at[j, kb(x)], ws.at[1, j], wr.at[1, j], dev(zh, across(j), core, zl, y))

    def w_far(j):
        block = wbuf.at[j, kb(across(j))]
        return remote(block, block, ws.at[2, j], wr.at[2, j], dev(zh, beside(j), core, zl, y))

    def w_pair(j, k):
        block = wbuf.at[j, kb((x + k) % 4)]
        return remote(block, block, ws.at[3 + k, j], wr.at[3 + k, j], dev(zh, x, 1 - core, zl, y))

    def w_send(j):
        load(j).wait()
        load_other(j).wait()
        w_beside(j).start()
        w_across(j).start()
        w_pair(j, 0).start()

    def t_x(sub):
        return remote(tok.at[at(sub, SUB)], txbuf.at[at(sub, SUB)], txs.at[sub], txr.at[sub], dev(zh, x2, core, zl, y))

    def t_z(e, sub, d):
        src = txbuf if e else tok
        return remote(src.at[at(sub, SUB)], tbuf.at[y, zh, e, at(sub, SUB)], tzs.at[e, sub, d], tzr.at[zh, e, sub],
                      dev(zl, x, core, d, y))

    def t_own(e, sub):
        src = txbuf if e else tok
        return pltpu.make_async_copy(src.at[at(sub, SUB)], tbuf.at[y, zh, e, at(sub, SUB)], tzr.at[zh, e, sub])

    def stays(d):
        return jnp.logical_and(zl == zh, zl == d)

    def t_along_z(e, sub):
        for d in (0, 1):
            @pl.when(stays(d))
            def _():
                t_own(e, sub).start()

            @pl.when(jnp.logical_not(stays(d)))
            def _():
                t_z(e, sub, d).start()

    def block_of(m):
        r = m // 2
        return jnp.where(r < 2, zo, zh), jnp.where((r == 1) | (r == 2), 1, 0)

    def t_piece(yy, m):
        z, e = block_of(m)
        return tbuf.at[yy, z, e, at(m % 2, SUB)]

    def t_near(m, k):
        piece = t_piece(y, m)
        return remote(piece, piece, tys.at[k, m], tyr.at[k, m], dev(zh, x, core, zl, (y + 1 + 2 * k) % 4))

    def t_next(m, k):
        z, e = block_of(m)
        piece = tbuf.at[(y + 3 - 2 * k) % 4, z, e, at((m % 2) * 2 + k, SUB // 2)]
        return remote(piece, piece, tys.at[2 + k, m], tyr.at[2 + k, m], dev(zh, x, core, zl, (y + 1 + 2 * k) % 4))

    def t_along_y(m):
        z, e = block_of(m)
        piece = t_piece(y, m)
        pltpu.make_async_copy(piece, piece, tzr.at[z, e, m % 2]).wait()
        t_near(m, 0).start()
        t_near(m, 1).start()

    for sub in (0, 1):
        t_x(sub).start()
        t_along_z(0, sub)

    w_send(0)
    w_send(1)

    iota = lambda shape, axis: lax.broadcasted_iota(jnp.int32, shape, axis)
    dot = lambda a, b, dims: lax.dot_general(a, b, (dims, ((), ())), preferred_element_type=F32)
    names = jnp.broadcast_to(owners[...], (32, 128))
    onehot = (names == iota((32, 128), 1)).astype(F32)
    before = (iota((32, 32), 1) < iota((32, 32), 0)).astype(BF16)
    earlier = dot(before, onehot.astype(BF16), ((1,), (0,)))
    slot = jnp.sum(earlier * onehot, axis=1, keepdims=True)
    mine[...] = jnp.broadcast_to(owners[...].astype(F32) * 2.0 + slot, (32, 128)).astype(BF16)

    def m_copy():
        return remote(mine, theirs, ms, mr, dev(zh, x2, core, zl, y))

    m_copy().start()
    t_along_y(0)
    t_x(0).wait_recv()
    t_along_z(1, 0)
    t_along_y(1)
    t_x(1).wait_recv()
    t_along_z(1, 1)

    def order(target):
        place = (target[:, :32].astype(F32) == iota((32, 32), 1).astype(F32)).astype(BF16)
        spread = (iota((ROWS, 32), 0) // 8 == iota((ROWS, 32), 1)).astype(BF16)
        part = dot(spread, place, ((1,), (1,))).astype(BF16)
        whole = dot(part, spread, ((1,), (1,)))
        same = (iota((ROWS, ROWS), 0) % 8 == iota((ROWS, ROWS), 1) % 8).astype(F32)
        return (whole * same).astype(BF16)

    sel[0] = order(mine[...])
    m_copy().wait_recv()
    sel[1] = order(theirs[...])

    lag = iota((128, LANES), 0)

    @pl.loop(0, CHUNKS)
    def _(j):
        cols = at(2 * j + group(j), LANES)
        value = taps_in[:, cols] * jnp.exp(-decay[:, cols] * lag.astype(F32))
        taps[j] = value + jnp.where(lag == 0, skip[:, cols], 0.0)

    def matmul(j, z, e):
        def add(xx, total):
            for half in (0, 1):
                w = jnp.concatenate([wbuf[j, xx * 2 + half, p] for p in range(3)], axis=1)
                total = total + jnp.dot(tbuf[xx, z, e, :, half * HALF:(half + 1) * HALF], w,
                                        preferred_element_type=F32)
            return total
        return lax.fori_loop(0, 4, add, jnp.zeros((ROWS, 3 * LANES), F32))

    def o_copy(j, e):
        return remote(osend.at[j, e], orecv.at[j, e], os_.at[j, e], or_.at[j, e], dev(zo, x, core, zl, y))

    def h_copy(j, e):
        xe = (x + 2 * e) % 4
        to = beside(j)
        same = jnp.where((xe + 1) % 4 == to, 0, 1)
        to_x, to_zh = jnp.where(core == 0, x, to), jnp.where(core == 0, zh, (zh + xe // 3) % 2)
        to_e = jnp.where(core == 0, e, same)
        return remote(ubuf.at[j, e, pl.ds(128, 128)], hrecv.at[j, to_e], hs.at[j, e], hr.at[j, to_e],
                      dev(to_zh, to_x, 1 - core, zl, y))

    def p_copy(j, e, o):
        to, source = (s + o) % 16, (zh * 4 + (x + 2 * e) % 4) * 2 + core
        return remote(psend.at[j, e, at(to, 16)], pbuf.at[2 * j + group(j), at(source, 16)],
                      ps.at[j, e], pr.at[2 * j + group(j)], (to, c))

    def g_copy(j):
        return remote(gsend.at[j], grecv.at[j], gs.at[j], gr.at[j], dev(zh, x2, core, zl, y))

    def stage_other(n):
        e = jnp.where(n < 6, n // 3, n - 6)
        j = jnp.where(n < 6, n % 3, 3)
        osend[j, e] = matmul(j, zo, e).astype(BF16)
        o_copy(j, e).start()

    def stage_u(j, e):
        own = matmul(j, zh, e)
        o_copy(j, e).wait_recv()
        full = (own + orecv[j, e].astype(F32)).astype(BF16)
        qbuf[j, e] = full[:, :LANES]
        u = (full[:, LANES:2 * LANES].astype(F32) * full[:, 2 * LANES:].astype(F32)).astype(BF16)
        ubuf[j, e] = u
        h_copy(j, e).start()
        psend[j, e] = jnp.dot(sel[e], u, preferred_element_type=F32).astype(BF16)

        @pl.loop(1, 16)
        def _(o):
            p_copy(j, e, o).start()

        source = (zh * 4 + (x + 2 * e) % 4) * 2 + core
        pbuf[2 * j + group(j), at(source, 16)] = psend[j, e, at(s, 16)]

    def stage_filter(j, e):
        pltpu.make_async_copy(hrecv.at[j, e], hrecv.at[j, e], hr.at[j, e]).wait()
        first = (zh == 0) & (core == 0) & ((x + 2 * e) % 4 == 0)
        prior = jnp.where(first, 0.0, hrecv[j, e].astype(F32))
        ext = jnp.concatenate([prior, ubuf[j, e].astype(F32)], axis=0)
        for b in range(8):
            shifts[b] = ext[8 - b:384 - b]

        def add(a, total):
            rows = taps[j, at(a, 8)]
            for b in range(8):
                total = total + rows[b:b + 1] * shifts[b, pl.ds(pl.multiple_of(120 - a * 8, 8), ROWS)]
            return total

        z = lax.fori_loop(0, 16, add, jnp.zeros((ROWS, LANES), F32))
        out = (qbuf[j, e].astype(F32) * z).astype(BF16)

        @pl.when(e == 1)
        def _():
            gsend[j] = out
            g_copy(j).start()

        @pl.when(e == 0)
        def _():
            gated[:, at(2 * j + group(j), LANES)] = out

    def others_done(i):
        return jnp.where(i < 2, 0, jnp.where(i < 4, i - 1, jnp.where(i == 4, 6, 8)))

    @pl.loop(0, MESSAGES + 1)
    def _(i):
        @pl.when((i >= 1) & (i <= 4))
        def _():
            j = i - 1
            w_across(j).wait_recv()
            w_far(j).start()
            w_pair(j, (across(j) + 4 - x) % 4).start()
            w_beside(j).wait_recv()
            w_pair(j, (beside(j) + 4 - x) % 4).start()

            @pl.when(j + 2 < CHUNKS)
            def _():
                w_send(j + 2)

        @pl.when(i < MESSAGES)
        def _():
            t_near(i, 0).wait_recv()
            t_next(i, 0).start()
            t_near(i, 1).wait_recv()
            t_next(i, 1).start()

        @pl.when(i + 2 < MESSAGES)
        def _():
            t_along_y(i + 2)

        @pl.when((i >= 2) & (i <= 5))
        def _():
            w_far(i - 2).wait_recv()
            w_pair(i - 2, 2).start()

        @pl.when(i >= 1)
        def _():
            t_next(i - 1, 0).wait_recv()
            t_next(i - 1, 1).wait_recv()

        @pl.when((i >= 2) & (i <= 5))
        def _():
            for k in range(4):
                w_pair(i - 2, k).wait_recv()

        @pl.loop(others_done(i - 1), others_done(i))
        def _(n):
            stage_other(n)

        @pl.when((i == 6) | (i == 8))
        def _():
            @pl.loop(0, jnp.where(i == 6, 4, 9))
            def _(t):
                @pl.when(t < 4)
                def _():
                    stage_u(t, jnp.where(i == 6, 1, 0))

                @pl.when((i == 8) & (t >= 1))
                def _():
                    stage_filter((t - 1) % 4, jnp.where(t <= 4, 1, 0))

    @pl.loop(0, CHUNKS)
    def _(j):
        few = pbuf.at[0, pl.ds(0, 224)]
        some = pbuf.at[0, pl.ds(0, 240)]
        all_ = pbuf.at[0]
        this, that = 2 * j + group(j), 2 * j + 1 - group(j)
        pltpu.make_async_copy(few, few, pr.at[this]).wait()
        pltpu.make_async_copy(all_, all_, pr.at[that]).wait()
        handed[:, at(this, LANES)] = pbuf[this]
        handed[:, at(that, LANES)] = pbuf[that]
        g_copy(j).wait_recv()
        gated[:, at(that, LANES)] = grecv[j]
        g_copy(j).wait_send()
        for e in (0, 1):
            pltpu.make_async_copy(some, some, ps.at[j, e]).wait()
            o_copy(j, e).wait_send()
            h_copy(j, e).wait_send()
        w_beside(j).wait_send()
        w_across(j).wait_send()
        w_far(j).wait_send()
        for k in range(4):
            w_pair(j, k).wait_send()

    @pl.loop(0, MESSAGES)
    def _(m):
        for k in (0, 1):
            t_near(m, k).wait_send()
            t_next(m, k).wait_send()

    m_copy().wait_send()
    for sub in (0, 1):
        t_x(sub).wait_send()
        for d in (0, 1):
            @pl.when(jnp.logical_not(stays(d)))
            def _():
                t_z(0, sub, d).wait_send()
                t_z(1, sub, d).wait_send()


def per_device(tokens, input_weight, filter_taps, decay_rates, skip_gain, owners):
    dma = pltpu.SemaphoreType.DMA
    vmem, any_ = pl.BlockSpec(memory_space=pltpu.VMEM), pl.BlockSpec(memory_space=pl.ANY)
    gated, handed = pl.pallas_call(
        kernel,
        out_shape=(jax.ShapeDtypeStruct((ROWS, 1024), BF16), jax.ShapeDtypeStruct((ROWS, 1024), BF16)),
        in_specs=[any_, any_, vmem, vmem, vmem, vmem],
        out_specs=(vmem, vmem),
        scratch_shapes=[
            pltpu.VMEM((CHUNKS, 8, 3, HALF, LANES), BF16),
            pltpu.VMEM((CHUNKS, 3, HALF, LANES), BF16),
            pltpu.VMEM((4, 2, 2, ROWS, 1024), BF16),
            pltpu.VMEM((ROWS, 1024), BF16),
            pltpu.VMEM((CHUNKS, 2, ROWS, 3 * LANES), BF16),
            pltpu.VMEM((CHUNKS, 2, ROWS, 3 * LANES), BF16),
            pltpu.VMEM((CHUNKS, 2, ROWS, LANES), BF16),
            pltpu.VMEM((CHUNKS, 2, ROWS, LANES), BF16),
            pltpu.VMEM((CHUNKS, 2, 128, LANES), BF16),
            pltpu.VMEM((CHUNKS, 2, ROWS, LANES), BF16),
            pltpu.VMEM((2 * CHUNKS, ROWS, LANES), BF16),
            pltpu.VMEM((CHUNKS, ROWS, LANES), BF16),
            pltpu.VMEM((CHUNKS, ROWS, LANES), BF16),
            pltpu.VMEM((32, 128), BF16),
            pltpu.VMEM((32, 128), BF16),
            pltpu.VMEM((2, ROWS, ROWS), BF16),
            pltpu.VMEM((CHUNKS, 128, LANES), F32),
            pltpu.VMEM((8, 376, LANES), F32),
            dma((2, CHUNKS)), dma((7, CHUNKS)), dma((7, CHUNKS)),
            dma((2,)), dma((2,)), dma((2, 2, 2)), dma((2, 2, 2)),
            dma((4, MESSAGES)), dma((4, MESSAGES)),
            dma((CHUNKS, 2)), dma((CHUNKS, 2)), dma((CHUNKS, 2)), dma((CHUNKS, 2)),
            dma((CHUNKS, 2)), dma((2 * CHUNKS,)), dma((CHUNKS,)), dma((CHUNKS,)), dma, dma,
        ],
        compiler_params=pltpu.CompilerParams(
            collective_id=0, has_side_effects=True, vmem_limit_bytes=56 * 1024 * 1024),
        name="hyena",
    )(tokens, input_weight, filter_taps, decay_rates.reshape(1, -1), skip_gain.reshape(1, -1), owners)
    return gated, handed.reshape(32, 8, 1024)


def solution(mesh):
    return jax.shard_map(
        per_device,
        mesh=mesh,
        in_specs=(P("seq", "chan"), P(None, "seq", "chan"), P(None, "chan"), P("chan"), P("chan"), P("seq", None)),
        out_specs=(P("seq", "chan"), P("seq", None, "chan")),
        check_vma=False,
    )
```

time: 561 us -> 146 us (0.26)
  waiting for transfers between devices: 381 us -> 0 us
  Pallas kernels: 0 us -> 139 us
  other arithmetic: 65.8 us -> 0 us
  blocking collectives: 58.2 us -> 0 us
  matrix products: 23.5 us -> 0 us
  between operations: 14.2 us -> 0.64 us
  starting transfers between devices: 8.25 us -> 0 us
    reduce_scatter x1 -> x0, waiting for transfers between devices: 323 us -> none  [per_device(): lax.psum_scatter(jnp.einsum('xy,iyz->xiz', rows_grouped, input_weight, pr...]
    pallas_call x0 -> x1, Pallas kernels: none -> 139 us  [per_device(): pl.pallas_call(kernel, out_shape=(jax.ShapeDtypeStruct((ROWS, 1024), BF16...]
    all_to_all x1 -> x0, blocking collectives: 58.2 us -> none  [per_device(): lax.all_to_all(whole, 'seq', split_axis=1, concat_axis=0, tiled=True)]
    all_gather x1 -> x0, waiting for transfers between devices: 56.9 us -> none  [per_device(): whole = lax.all_gather(tokens, 'chan', axis=1, tiled=True)]
    add x17 -> x0, other arithmetic: 56.6 us -> none  [the longest x16 56.6 us: add_group(): total = total + weight_row * shifted]
    dot_general x2 -> x0, matrix products: 23.5 us -> none  [the longest x1 22.7 us: per_device(): jnp.einsum('xy,iyz->xiz', rows_grouped, input_weight, preferred_element_t...]
    convert_element_type x6 -> x0, other arithmetic: 8.83 us -> none  [the longest x3 5.02 us: per_device(): (key_part.astype(jnp.float32) * value_slice.astype(jnp.float32)).astype(j...]
    all_to_all x1 -> x0, starting transfers between devices: 6.87 us -> none  [handoff_page_list(): lax.all_to_all(buffer, 'seq', split_axis=0, concat_axis=0, tiled=True)]
  transfers between devices with their start and end apart: 4 -> 0, of which waited for: 2 -> 0; matrix products, arithmetic and copies ran while one was open for 12% -> 0% of each run, Pallas kernels for 0% -> 0%
where the time goes in v2:
time: 146 us; the launch traced here: 144 us
  Pallas kernels  139 us (95%)
  local copies, waits for them, and re-layouts  5.08 us (3%)
    pallas_call x1, Pallas kernels, per_device(): pl.pallas_call(kernel, out_shape=(jax.ShapeDtypeStruct((ROWS, 1024), BF16...  139 us
    unnamed x3, local copies, waits for them, and re-layouts  5.08 us

profile of v2, /device:TPU:0, one launch (start us, length us, event | category | flops | bytes accessed | tf_op | source)
XLA Modules:
  0.0 144.3 jit_solution(308876519115056787)
XLA Ops:
  0.6 1.3 copy.8.owners
  2.0 138.6 %hyena.1 = (bf16[256,1024]{1,0:T(8,128)(2,1)}, bf16[256,1024]{1,0:T(8,128)(2,1)}) custom-call(bf16[256,1024]{1,0:T(8,128)(2,1)} %tok.1, bf16[3,512,1024]{2,1,0:T(8,128)(2,1)} %wgt.1, f32[128,1024]{1,0:T(8,128)} %taps_in.1, f32[1,1024]{1,0:T(1,128)} %bitcast.4, f32[1,1024]{1,0:T(1,128)} %bitcast.5, s32[32,1]{1,0:T(8,128)} %copy.8.owners), custom_call_target="tpu_custom_call" | custom-call | tf_op jit(solution)/shard_map/hyena/pallas_call | solution.py:368
  140.6 1.9 %copy.11 = bf16[256,1024]{1,0:T(8,128)(2,1)} copy(bf16[256,1024]{1,0:T(8,128)(2,1)} %get-tuple-element.8) | data formatting | bytes 1048576
  142.5 1.9 %copy.12 = bf16[32,8,1024]{2,1,0:T(8,128)(2,1)} copy(bf16[32,8,1024]{2,1,0:T(8,128)(2,1)} %bitcast.3) | data formatting | bytes 1048576

commit v3 on v2

--- a/solution.py
+++ b/solution.py
@@ -8,12 +8,14 @@
 MESH = pl.DeviceIdType.MESH
 F32, BF16 = jnp.float32, jnp.bfloat16
 CHUNKS, LANES = 4, 128
-ROWS, HALF, SUB = 256, 512, 128
-MESSAGES = 8
+ROWS, HALF = 256, 512
+PARTS = 4
+SUB, MESSAGES = ROWS // PARTS, 4 * PARTS
+AHEAD, UNITS, W_AHEAD, W_LEAD = 4, 3 * CHUNKS, 3, 1
 
 
 def kernel(tok, wgt, taps_in, decay, skip, owners, gated, handed,
-           wbuf, wother, tbuf, txbuf, osend, orecv, qbuf, ubuf, hrecv, psend, pbuf, gsend, grecv,
+           wbuf, wother, tbuf, txbuf, own, osend, orecv, qbuf, ubuf, hrecv, psend, pbuf, gsend, grecv,
            mine, theirs, sel, taps, shifts,
            wl, ws, wr, txs, txr, tzs, tzr, tys, tyr, os_, or_, hs, hr, ps, pr, gs, gr, ms, mr):
     s, c = lax.axis_index("seq"), lax.axis_index("chan")
@@ -58,36 +60,57 @@
 
     barrier = pltpu.get_barrier_semaphore()
 
-    @pl.loop(1, 16)
-    def _(o):
-        pl.semaphore_signal(barrier, inc=1, device_id=((s + o) % 16, c), device_id_type=MESH)
-
-    for dy in (1, 2, 3):
-        pl.semaphore_signal(barrier, inc=1, device_id=dev(zh, x, core, zl, (y + dy) % 4), device_id_type=MESH)
-    for z in (0, 1):
-        pl.semaphore_signal(barrier, inc=1, device_id=dev(z, x, core, 1 - zl, y), device_id_type=MESH)
-    pl.semaphore_wait(barrier, 20)
-
-    def w_beside(j):
-        return remote(wbuf.at[j, kb(x)], wbuf.at[j, kb(x)], ws.at[0, j], wr.at[0, j], dev(zh, beside(j), core, zl, y))
-
-    def w_across(j):
-        return remote(wother.at[j], wbuf.at[j, kb(x)], ws.at[1, j], wr.at[1, j], dev(zh, across(j), core, zl, y))
-
-    def w_far(j):
-        block = wbuf.at[j, kb(across(j))]
-        return remote(block, block, ws.at[2, j], wr.at[2, j], dev(zh, beside(j), core, zl, y))
+    partners = [dev(zh, (x + d) % 4, core, zl, y) for d in (1, 2, 3)] + [dev(zh, x, 1 - core, zl, y)]
+    partners += [dev(zo, x, core, zl, y), dev(zh, x, core, 1 - zl, y), dev(zo, x, core, 1 - zl, y)]
+    partners += [dev(zh, x, core, zl, (y + d) % 4) for d in (1, 3)]
+    for partner in partners:
+        pl.semaphore_signal(barrier, inc=1, device_id=partner, device_id_type=MESH)
+    pl.semaphore_wait(barrier, len(partners))
+
+    def w_beside(v):
+        block = wbuf.at[v // 3, kb(x), v % 3]
+        return remote(block, block, ws.at[0, v], wr.at[0, v], dev(zh, beside(v // 3), core, zl, y))
+
+    def w_across(v):
+        return remote(wother.at[v // 3, v % 3], wbuf.at[v // 3, kb(x), v % 3], ws.at[1, v], wr.at[1, v],
+                      dev(zh, across(v // 3), core, zl, y))
+
+    def w_far(v):
+        block = wbuf.at[v // 3, kb(across(v // 3)), v % 3]
+        return remote(block, block, ws.at[2, v], wr.at[2, v], dev(zh, beside(v // 3), core, zl, y))
 
     def w_pair(j, k):
         block = wbuf.at[j, kb((x + k) % 4)]
         return remote(block, block, ws.at[3 + k, j], wr.at[3 + k, j], dev(zh, x, 1 - core, zl, y))
 
-    def w_send(j):
-        load(j).wait()
-        load_other(j).wait()
-        w_beside(j).start()
-        w_across(j).start()
-        w_pair(j, 0).start()
+    def w_send(v):
+        @pl.when(v % 3 == 0)
+        def _():
+            load(v // 3).wait()
+            load_other(v // 3).wait()
+
+        w_beside(v).start()
+        w_across(v).start()
+
+    def w_step(v):
+        @pl.when(v < UNITS)
+        def _():
+            w_across(v).wait_recv()
+            w_far(v).start()
+            w_beside(v).wait_recv()
+
+            @pl.when(v + W_AHEAD < UNITS)
+            def _():
+                w_send(v + W_AHEAD)
+
+        @pl.when((v >= 1) & (v <= UNITS))
+        def _():
+            w_far(v - 1).wait_recv()
+
+            @pl.when(v % 3 == 0)
+            def _():
+                for k in range(4):
+                    w_pair(v // 3 - 1, k).start()
 
     def t_x(sub):
         return remote(tok.at[at(sub, SUB)], txbuf.at[at(sub, SUB)], txs.at[sub], txr.at[sub], dev(zh, x2, core, zl, y))
@@ -114,13 +137,15 @@
             def _():
                 t_z(e, sub, d).start()
 
+    early = x // 2
+
     def block_of(m):
-        r = m // 2
-        return jnp.where(r < 2, zo, zh), jnp.where((r == 1) | (r == 2), 1, 0)
+        r = m // PARTS
+        return jnp.where(r < 2, zo, zh), jnp.where(r < 2, r, (early + r) % 2)
 
     def t_piece(yy, m):
         z, e = block_of(m)
-        return tbuf.at[yy, z, e, at(m % 2, SUB)]
+        return tbuf.at[yy, z, e, at(m % PARTS, SUB)]
 
     def t_near(m, k):
         piece = t_piece(y, m)
@@ -128,47 +153,50 @@
 
     def t_next(m, k):
         z, e = block_of(m)
-        piece = tbuf.at[(y + 3 - 2 * k) % 4, z, e, at((m % 2) * 2 + k, SUB // 2)]
+        piece = tbuf.at[(y + 3 - 2 * k) % 4, z, e, at((m % PARTS) * 2 + k, SUB // 2)]
         return remote(piece, piece, tys.at[2 + k, m], tyr.at[2 + k, m], dev(zh, x, core, zl, (y + 1 + 2 * k) % 4))
 
     def t_along_y(m):
         z, e = block_of(m)
         piece = t_piece(y, m)
-        pltpu.make_async_copy(piece, piece, tzr.at[z, e, m % 2]).wait()
+        pltpu.make_async_copy(piece, piece, tzr.at[z, e, m % PARTS]).wait()
         t_near(m, 0).start()
         t_near(m, 1).start()
 
-    for sub in (0, 1):
+    for sub in range(PARTS):
         t_x(sub).start()
+    for sub in range(PARTS):
         t_along_z(0, sub)
-
-    w_send(0)
-    w_send(1)
+    for v in range(W_AHEAD):
+        w_send(v)
 
     iota = lambda shape, axis: lax.broadcasted_iota(jnp.int32, shape, axis)
     dot = lambda a, b, dims: lax.dot_general(a, b, (dims, ((), ())), preferred_element_type=F32)
-    names = jnp.broadcast_to(owners[...], (32, 128))
-    onehot = (names == iota((32, 128), 1)).astype(F32)
-    before = (iota((32, 32), 1) < iota((32, 32), 0)).astype(BF16)
-    earlier = dot(before, onehot.astype(BF16), ((1,), (0,)))
-    slot = jnp.sum(earlier * onehot, axis=1, keepdims=True)
-    mine[...] = jnp.broadcast_to(owners[...].astype(F32) * 2.0 + slot, (32, 128)).astype(BF16)
+    onehot = (jnp.broadcast_to(owners[...], (32, 32)) == iota((32, 32), 0)).astype(F32)
+    before = (iota((32, 32), 0) < iota((32, 32), 1)).astype(BF16)
+    earlier = dot(onehot.astype(BF16), before, ((1,), (0,)))
+    target = owners[...].astype(F32) * 2.0 + jnp.sum(earlier * onehot, axis=0, keepdims=True)
+    place = (jnp.broadcast_to(target, (32, 32)) == iota((32, 32), 0).astype(F32)).astype(F32)
+    mine[...] = jnp.concatenate([place, jnp.zeros((32, 96), F32)], axis=1).astype(BF16)
 
     def m_copy():
         return remote(mine, theirs, ms, mr, dev(zh, x2, core, zl, y))
 
     m_copy().start()
     t_along_y(0)
-    t_x(0).wait_recv()
-    t_along_z(1, 0)
     t_along_y(1)
-    t_x(1).wait_recv()
-    t_along_z(1, 1)
-
-    def order(target):
-        place = (target[:, :32].astype(F32) == iota((32, 32), 1).astype(F32)).astype(BF16)
+    w_step(0)
+    for sub in range(PARTS):
+        t_x(sub).wait_recv()
+        t_along_z(1, sub)
+        if sub + 2 < AHEAD:
+            t_along_y(sub + 2)
+        if sub + 1 < W_LEAD:
+            w_step(sub + 1)
+
+    def order(place):
         spread = (iota((ROWS, 32), 0) // 8 == iota((ROWS, 32), 1)).astype(BF16)
-        part = dot(spread, place, ((1,), (1,))).astype(BF16)
+        part = dot(spread, place[:, :32], ((1,), (0,))).astype(BF16)
         whole = dot(part, spread, ((1,), (1,)))
         same = (iota((ROWS, ROWS), 0) % 8 == iota((ROWS, ROWS), 1) % 8).astype(F32)
         return (whole * same).astype(BF16)
@@ -186,13 +214,9 @@
         taps[j] = value + jnp.where(lag == 0, skip[:, cols], 0.0)
 
     def matmul(j, z, e):
-        def add(xx, total):
-            for half in (0, 1):
-                w = jnp.concatenate([wbuf[j, xx * 2 + half, p] for p in range(3)], axis=1)
-                total = total + jnp.dot(tbuf[xx, z, e, :, half * HALF:(half + 1) * HALF], w,
-                                        preferred_element_type=F32)
-            return total
-        return lax.fori_loop(0, 4, add, jnp.zeros((ROWS, 3 * LANES), F32))
+        t = jnp.concatenate([tbuf[yy, z, e] for yy in range(4)], axis=1)
+        w = jnp.concatenate([jnp.concatenate([wbuf[j, k, p] for k in range(8)], axis=0) for p in range(3)], axis=1)
+        return jnp.dot(t, w, preferred_element_type=F32)
 
     def o_copy(j, e):
         return remote(osend.at[j, e], orecv.at[j, e], os_.at[j, e], or_.at[j, e], dev(zo, x, core, zl, y))
@@ -215,15 +239,17 @@
         return remote(gsend.at[j], grecv.at[j], gs.at[j], gr.at[j], dev(zh, x2, core, zl, y))
 
     def stage_other(n):
-        e = jnp.where(n < 6, n // 3, n - 6)
-        j = jnp.where(n < 6, n % 3, 3)
+        e = jnp.where(n < 2, 0, jnp.where(n < 4, 1, n % 2))
+        j = jnp.where(n < 2, n, jnp.where(n < 4, n - 2, n // 2))
         osend[j, e] = matmul(j, zo, e).astype(BF16)
         o_copy(j, e).start()
 
+    def stage_own(j, e):
+        own[j] = matmul(j, zh, e)
+
     def stage_u(j, e):
-        own = matmul(j, zh, e)
         o_copy(j, e).wait_recv()
-        full = (own + orecv[j, e].astype(F32)).astype(BF16)
+        full = (own[j] + orecv[j, e].astype(F32)).astype(BF16)
         qbuf[j, e] = full[:, :LANES]
         u = (full[:, LANES:2 * LANES].astype(F32) * full[:, 2 * LANES:].astype(F32)).astype(BF16)
         ubuf[j, e] = u
@@ -245,13 +271,29 @@
         for b in range(8):
             shifts[b] = ext[8 - b:384 - b]
 
-        def add(a, total):
-            rows = taps[j, at(a, 8)]
-            for b in range(8):
-                total = total + rows[b:b + 1] * shifts[b, pl.ds(pl.multiple_of(120 - a * 8, 8), ROWS)]
-            return total
-
-        z = lax.fori_loop(0, 16, add, jnp.zeros((ROWS, LANES), F32))
+        def stream(count, tap, data):
+            def add(b, sums):
+                x_ = [data(b, m) for m in range(count + 7)]
+                sums = list(sums)
+                for a in range(8):
+                    weight = jnp.broadcast_to(tap(b, a), (8, LANES))
+                    for r in range(count):
+                        sums[r] = sums[r] + weight * x_[r - a + 7]
+                return tuple(sums)
+            return lax.fori_loop(0, 8, add, tuple(jnp.zeros((8, LANES), F32) for _ in range(count)), unroll=2)
+
+        def rows_of(b, m):
+            return shifts[b, 8 * m:8 * m + 8]
+
+        def tap_of(b, a):
+            return taps[j, pl.ds(8 * a + b, 1)]
+
+        even = stream(16, lambda b, a: tap_of(b, 2 * a), lambda b, m: rows_of(b, 2 * m + 1))
+        odd = stream(17, lambda b, a: tap_of(b, 2 * a + 1), lambda b, m: rows_of(b, 2 * m))
+        both = stream(16, lambda b, a: tap_of(b, 2 * a) + tap_of(b, 2 * a + 1),
+                      lambda b, m: rows_of(b, 2 * m + 1) + rows_of(b, 2 * m + 2))
+        z = jnp.concatenate(
+            [piece for r in range(16) for piece in (even[r] + odd[r], both[r] - even[r] - odd[r + 1])], axis=0)
         out = (qbuf[j, e].astype(F32) * z).astype(BF16)
 
         @pl.when(e == 1)
@@ -263,24 +305,20 @@
         def _():
             gated[:, at(2 * j + group(j), LANES)] = out
 
+    waits = (zh == 1) & (core == 0) & (x % 2 == 0)
+    now = jnp.where(waits, 0, 3)
+
     def others_done(i):
-        return jnp.where(i < 2, 0, jnp.where(i < 4, i - 1, jnp.where(i == 4, 6, 8)))
+        return jnp.where(i < 4, 0, jnp.where(i < 8, i // 2 - 1, jnp.where(i < 11, i - 4, jnp.where(i < 12, 6, 8))))
+
+    def owns_done(i):
+        return jnp.where(i < 13, 0, jnp.where(i == 13, 2, jnp.where(i < 16, 3, 8)))
+
+    def filters_done(i):
+        return jnp.where(i < 14, 0, jnp.where(i == 14, jnp.minimum(now, 1), jnp.where(i == 15, now, 8)))
 
     @pl.loop(0, MESSAGES + 1)
     def _(i):
-        @pl.when((i >= 1) & (i <= 4))
-        def _():
-            j = i - 1
-            w_across(j).wait_recv()
-            w_far(j).start()
-            w_pair(j, (across(j) + 4 - x) % 4).start()
-            w_beside(j).wait_recv()
-            w_pair(j, (beside(j) + 4 - x) % 4).start()
-
-            @pl.when(j + 2 < CHUNKS)
-            def _():
-                w_send(j + 2)
-
         @pl.when(i < MESSAGES)
         def _():
             t_near(i, 0).wait_recv()
@@ -288,40 +326,37 @@
             t_near(i, 1).wait_recv()
             t_next(i, 1).start()
 
-        @pl.when(i + 2 < MESSAGES)
-        def _():
-            t_along_y(i + 2)
-
-        @pl.when((i >= 2) & (i <= 5))
-        def _():
-            w_far(i - 2).wait_recv()
-            w_pair(i - 2, 2).start()
+        @pl.when(i + AHEAD < MESSAGES)
+        def _():
+            t_along_y(i + AHEAD)
+
+        w_step(i + W_LEAD)
+
+        done = i + W_LEAD - 4
+
+        @pl.when((done >= 0) & (done <= 9) & (done % 3 == 0))
+        def _():
+            for k in range(4):
+                w_pair(done // 3, k).wait_recv()
 
         @pl.when(i >= 1)
         def _():
             t_next(i - 1, 0).wait_recv()
             t_next(i - 1, 1).wait_recv()
-
-        @pl.when((i >= 2) & (i <= 5))
-        def _():
-            for k in range(4):
-                w_pair(i - 2, k).wait_recv()
 
         @pl.loop(others_done(i - 1), others_done(i))
         def _(n):
             stage_other(n)
 
-        @pl.when((i == 6) | (i == 8))
-        def _():
-            @pl.loop(0, jnp.where(i == 6, 4, 9))
-            def _(t):
-                @pl.when(t < 4)
-                def _():
-                    stage_u(t, jnp.where(i == 6, 1, 0))
-
-                @pl.when((i == 8) & (t >= 1))
-                def _():
-                    stage_filter((t - 1) % 4, jnp.where(t <= 4, 1, 0))
+        @pl.loop(owns_done(i - 1), owns_done(i))
+        def _(n):
+            e = jnp.where(n >= CHUNKS, 1 - early, early)
+            stage_own(n % CHUNKS, e)
+            stage_u(n % CHUNKS, e)
+
+        @pl.loop(filters_done(i - 1), filters_done(i))
+        def _(n):
+            stage_filter(n % CHUNKS, jnp.where(n < CHUNKS, early, 1 - early))
 
     @pl.loop(0, CHUNKS)
     def _(j):
@@ -340,11 +375,14 @@
             pltpu.make_async_copy(some, some, ps.at[j, e]).wait()
             o_copy(j, e).wait_send()
             h_copy(j, e).wait_send()
-        w_beside(j).wait_send()
-        w_across(j).wait_send()
-        w_far(j).wait_send()
         for k in range(4):
             w_pair(j, k).wait_send()
+
+    @pl.loop(0, UNITS)
+    def _(v):
+        w_beside(v).wait_send()
+        w_across(v).wait_send()
+        w_far(v).wait_send()
 
     @pl.loop(0, MESSAGES)
     def _(m):
@@ -353,7 +391,7 @@
             t_next(m, k).wait_send()
 
     m_copy().wait_send()
-    for sub in (0, 1):
+    for sub in range(PARTS):
         t_x(sub).wait_send()
         for d in (0, 1):
             @pl.when(jnp.logical_not(stays(d)))
@@ -375,6 +413,7 @@
             pltpu.VMEM((CHUNKS, 3, HALF, LANES), BF16),
             pltpu.VMEM((4, 2, 2, ROWS, 1024), BF16),
             pltpu.VMEM((ROWS, 1024), BF16),
+            pltpu.VMEM((CHUNKS, ROWS, 3 * LANES), F32),
             pltpu.VMEM((CHUNKS, 2, ROWS, 3 * LANES), BF16),
             pltpu.VMEM((CHUNKS, 2, ROWS, 3 * LANES), BF16),
             pltpu.VMEM((CHUNKS, 2, ROWS, LANES), BF16),
@@ -389,8 +428,8 @@
             pltpu.VMEM((2, ROWS, ROWS), BF16),
             pltpu.VMEM((CHUNKS, 128, LANES), F32),
             pltpu.VMEM((8, 376, LANES), F32),
-            dma((2, CHUNKS)), dma((7, CHUNKS)), dma((7, CHUNKS)),
-            dma((2,)), dma((2,)), dma((2, 2, 2)), dma((2, 2, 2)),
+            dma((2, CHUNKS)), dma((7, UNITS)), dma((7, UNITS)),
+            dma((PARTS,)), dma((PARTS,)), dma((2, PARTS, 2)), dma((2, 2, PARTS)),
             dma((4, MESSAGES)), dma((4, MESSAGES)),
             dma((CHUNKS, 2)), dma((CHUNKS, 2)), dma((CHUNKS, 2)), dma((CHUNKS, 2)),
             dma((CHUNKS, 2)), dma((2 * CHUNKS,)), dma((CHUNKS,)), dma((CHUNKS,)), dma, dma,
@@ -398,7 +437,7 @@
         compiler_params=pltpu.CompilerParams(
             collective_id=0, has_side_effects=True, vmem_limit_bytes=56 * 1024 * 1024),
         name="hyena",
-    )(tokens, input_weight, filter_taps, decay_rates.reshape(1, -1), skip_gain.reshape(1, -1), owners)
+    )(tokens, input_weight, filter_taps, decay_rates.reshape(1, -1), skip_gain.reshape(1, -1), owners.reshape(1, -1))
     return gated, handed.reshape(32, 8, 1024)
 
 

time: 146 us -> 137 us (0.938)
  Pallas kernels: 139 us -> 132 us
    pallas_call x1, Pallas kernels: 139 us -> 132 us  [per_device(): pl.pallas_call(kernel, out_shape=(jax.ShapeDtypeStruct((ROWS, 1024), BF16...]
    unnamed x3 -> x2, local copies, waits for them, and re-layouts: 5.08 us -> 3.74 us
where the time goes in v3:
time: 137 us; the launch traced here: 136 us
  Pallas kernels  132 us (96%)
  local copies, waits for them, and re-layouts  3.74 us (3%)
    pallas_call x1, Pallas kernels, per_device(): pl.pallas_call(kernel, out_shape=(jax.ShapeDtypeStruct((ROWS, 1024), BF16...  132 us
    unnamed x2, local copies, waits for them, and re-layouts  3.74 us

profile of v3, /device:TPU:0, one launch (start us, length us, event | category | flops | bytes accessed | tf_op | source)
XLA Modules:
  0.0 136.2 jit_solution(17680687823479411116)
XLA Ops:
  0.6 131.8 %hyena.1 = (bf16[256,1024]{1,0:T(8,128)(2,1)}, bf16[256,1024]{1,0:T(8,128)(2,1)}) custom-call(bf16[256,1024]{1,0:T(8,128)(2,1)} %tok.1, bf16[3,512,1024]{2,1,0:T(8,128)(2,1)} %wgt.1, f32[128,1024]{1,0:T(8,128)} %taps_in.1, f32[1,1024]{1,0:T(1,128)} %bitcast.5, f32[1,1024]{1,0:T(1,128)} %bitcast.6, s32[1,32]{1,0:T(1,128)} %bitcast.7), custom_call_target="tpu_custom_call" | custom-call | tf_op jit(solution)/shard_map/hyena/pallas_call | solution.py:406
  132.4 1.9 %copy.10 = bf16[256,1024]{1,0:T(8,128)(2,1)} copy(bf16[256,1024]{1,0:T(8,128)(2,1)} %get-tuple-element.8) | data formatting | bytes 1048576
  134.3 1.9 %copy.11 = bf16[32,8,1024]{2,1,0:T(8,128)(2,1)} copy(bf16[32,8,1024]{2,1,0:T(8,128)(2,1)} %bitcast.4) | data formatting | bytes 1048576

commit v4 on v3

--- a/solution.py
+++ b/solution.py
@@ -69,19 +69,19 @@
 
     def w_beside(v):
         block = wbuf.at[v // 3, kb(x), v % 3]
-        return remote(block, block, ws.at[0, v], wr.at[0, v], dev(zh, beside(v // 3), core, zl, y))
+        return remote(block, block, ws.at[0], wr.at[0, v], dev(zh, beside(v // 3), core, zl, y))
 
     def w_across(v):
-        return remote(wother.at[v // 3, v % 3], wbuf.at[v // 3, kb(x), v % 3], ws.at[1, v], wr.at[1, v],
+        return remote(wother.at[v // 3, v % 3], wbuf.at[v // 3, kb(x), v % 3], ws.at[0], wr.at[1, v],
                       dev(zh, across(v // 3), core, zl, y))
 
     def w_far(v):
         block = wbuf.at[v // 3, kb(across(v // 3)), v % 3]
-        return remote(block, block, ws.at[2, v], wr.at[2, v], dev(zh, beside(v // 3), core, zl, y))
+        return remote(block, block, ws.at[0], wr.at[2, v], dev(zh, beside(v // 3), core, zl, y))
 
     def w_pair(j, k):
         block = wbuf.at[j, kb((x + k) % 4)]
-        return remote(block, block, ws.at[3 + k, j], wr.at[3 + k, j], dev(zh, x, 1 - core, zl, y))
+        return remote(block, block, ws.at[1], wr.at[3 + k, j], dev(zh, x, 1 - core, zl, y))
 
     def w_send(v):
         @pl.when(v % 3 == 0)
@@ -113,11 +113,11 @@
                     w_pair(v // 3 - 1, k).start()
 
     def t_x(sub):
-        return remote(tok.at[at(sub, SUB)], txbuf.at[at(sub, SUB)], txs.at[sub], txr.at[sub], dev(zh, x2, core, zl, y))
+        return remote(tok.at[at(sub, SUB)], txbuf.at[at(sub, SUB)], txs.at[0], txr.at[sub], dev(zh, x2, core, zl, y))
 
     def t_z(e, sub, d):
         src = txbuf if e else tok
-        return remote(src.at[at(sub, SUB)], tbuf.at[y, zh, e, at(sub, SUB)], tzs.at[e, sub, d], tzr.at[zh, e, sub],
+        return remote(src.at[at(sub, SUB)], tbuf.at[y, zh, e, at(sub, SUB)], tzs.at[e, d], tzr.at[zh, e, sub],
                       dev(zl, x, core, d, y))
 
     def t_own(e, sub):
@@ -149,12 +149,12 @@
 
     def t_near(m, k):
         piece = t_piece(y, m)
-        return remote(piece, piece, tys.at[k, m], tyr.at[k, m], dev(zh, x, core, zl, (y + 1 + 2 * k) % 4))
+        return remote(piece, piece, tys.at[0], tyr.at[k, m], dev(zh, x, core, zl, (y + 1 + 2 * k) % 4))
 
     def t_next(m, k):
         z, e = block_of(m)
         piece = tbuf.at[(y + 3 - 2 * k) % 4, z, e, at((m % PARTS) * 2 + k, SUB // 2)]
-        return remote(piece, piece, tys.at[2 + k, m], tyr.at[2 + k, m], dev(zh, x, core, zl, (y + 1 + 2 * k) % 4))
+        return remote(piece, piece, tys.at[0], tyr.at[2 + k, m], dev(zh, x, core, zl, (y + 1 + 2 * k) % 4))
 
     def t_along_y(m):
         z, e = block_of(m)
@@ -219,7 +219,7 @@
         return jnp.dot(t, w, preferred_element_type=F32)
 
     def o_copy(j, e):
-        return remote(osend.at[j, e], orecv.at[j, e], os_.at[j, e], or_.at[j, e], dev(zo, x, core, zl, y))
+        return remote(osend.at[j, e], orecv.at[j, e], os_.at[0], or_.at[j, e], dev(zo, x, core, zl, y))
 
     def h_copy(j, e):
         xe = (x + 2 * e) % 4
@@ -227,16 +227,23 @@
         same = jnp.where((xe + 1) % 4 == to, 0, 1)
         to_x, to_zh = jnp.where(core == 0, x, to), jnp.where(core == 0, zh, (zh + xe // 3) % 2)
         to_e = jnp.where(core == 0, e, same)
-        return remote(ubuf.at[j, e, pl.ds(128, 128)], hrecv.at[j, to_e], hs.at[j, e], hr.at[j, to_e],
+        return remote(ubuf.at[j, e, pl.ds(128, 128)], hrecv.at[j, to_e], hs.at[0], hr.at[j, to_e],
                       dev(to_zh, to_x, 1 - core, zl, y))
 
-    def p_copy(j, e, o):
+    def p_copy(e, o):
         to, source = (s + o) % 16, (zh * 4 + (x + 2 * e) % 4) * 2 + core
-        return remote(psend.at[j, e, at(to, 16)], pbuf.at[2 * j + group(j), at(source, 16)],
-                      ps.at[j, e], pr.at[2 * j + group(j)], (to, c))
+        return remote(psend.at[e, :, at(to, 16)], pbuf.at[e, :, at(source, 16)], ps.at[e], pr.at[e], (to, c))
+
+    def stage_pages(e):
+        @pl.loop(1, 16)
+        def _(o):
+            p_copy(e, o).start()
+
+        source = (zh * 4 + (x + 2 * e) % 4) * 2 + core
+        pbuf[e, :, at(source, 16)] = psend[e, :, at(s, 16)]
 
     def g_copy(j):
-        return remote(gsend.at[j], grecv.at[j], gs.at[j], gr.at[j], dev(zh, x2, core, zl, y))
+        return remote(gsend.at[j], grecv.at[j], gs.at[0], gr.at[j], dev(zh, x2, core, zl, y))
 
     def stage_other(n):
         e = jnp.where(n < 2, 0, jnp.where(n < 4, 1, n % 2))
@@ -244,24 +251,30 @@
         osend[j, e] = matmul(j, zo, e).astype(BF16)
         o_copy(j, e).start()
 
-    def stage_own(j, e):
-        own[j] = matmul(j, zh, e)
-
-    def stage_u(j, e):
+    def stage_own(n):
+        late = n // 4
+        pair = jnp.where(n < 4, n // 2, n % 2)
+        rows = at(jnp.where(n < 4, n % 2, (n - 4) // 2), ROWS // 2)
+        e = jnp.where(n < 4, early, 1 - early)
+        t = jnp.concatenate([tbuf[yy, zh, e, rows] for yy in range(4)], axis=1)
+        w = jnp.concatenate([jnp.concatenate([wbuf[2 * pair + q, k, p] for k in range(8)], axis=0)
+                             for q in (0, 1) for p in range(3)], axis=1)
+        both = jnp.dot(t, w, preferred_element_type=F32)
+        for q in (0, 1):
+            own[late, 2 * pair + q, rows] = both[:, 3 * LANES * q:3 * LANES * (q + 1)]
+
+    def stage_u(j, e, late):
         o_copy(j, e).wait_recv()
-        full = (own[j] + orecv[j, e].astype(F32)).astype(BF16)
+        full = (own[late, j] + orecv[j, e].astype(F32)).astype(BF16)
         qbuf[j, e] = full[:, :LANES]
         u = (full[:, LANES:2 * LANES].astype(F32) * full[:, 2 * LANES:].astype(F32)).astype(BF16)
         ubuf[j, e] = u
         h_copy(j, e).start()
-        psend[j, e] = jnp.dot(sel[e], u, preferred_element_type=F32).astype(BF16)
-
-        @pl.loop(1, 16)
-        def _(o):
-            p_copy(j, e, o).start()
-
-        source = (zh * 4 + (x + 2 * e) % 4) * 2 + core
-        pbuf[2 * j + group(j), at(source, 16)] = psend[j, e, at(s, 16)]
+        psend[e, j] = jnp.dot(sel[e], u, preferred_element_type=F32).astype(BF16)
+
+        @pl.when(j == CHUNKS - 1)
+        def _():
+            stage_pages(e)
 
     def stage_filter(j, e):
         pltpu.make_async_copy(hrecv.at[j, e], hrecv.at[j, e], hr.at[j, e]).wait()
@@ -312,10 +325,13 @@
         return jnp.where(i < 4, 0, jnp.where(i < 8, i // 2 - 1, jnp.where(i < 11, i - 4, jnp.where(i < 12, 6, 8))))
 
     def owns_done(i):
+        return jnp.where(i < 13, 0, jnp.where(i < 16, 2 * (i - 12), 6))
+
+    def us_done(i):
         return jnp.where(i < 13, 0, jnp.where(i == 13, 2, jnp.where(i < 16, 3, 8)))
 
     def filters_done(i):
-        return jnp.where(i < 14, 0, jnp.where(i == 14, jnp.minimum(now, 1), jnp.where(i == 15, now, 8)))
+        return jnp.where(i < 16, 0, 8)
 
     @pl.loop(0, MESSAGES + 1)
     def _(i):
@@ -350,54 +366,54 @@
 
         @pl.loop(owns_done(i - 1), owns_done(i))
         def _(n):
-            e = jnp.where(n >= CHUNKS, 1 - early, early)
-            stage_own(n % CHUNKS, e)
-            stage_u(n % CHUNKS, e)
+            stage_own(n)
+
+        @pl.loop(us_done(i - 1), us_done(i))
+        def _(n):
+            late = n // CHUNKS
+
+            @pl.when((late == 1) & (n % 2 == 0))
+            def _():
+                stage_own(6 + n % CHUNKS // 2)
+
+            stage_u(n % CHUNKS, jnp.where(late == 1, 1 - early, early), late)
 
         @pl.loop(filters_done(i - 1), filters_done(i))
         def _(n):
             stage_filter(n % CHUNKS, jnp.where(n < CHUNKS, early, 1 - early))
 
-    @pl.loop(0, CHUNKS)
-    def _(j):
-        few = pbuf.at[0, pl.ds(0, 224)]
-        some = pbuf.at[0, pl.ds(0, 240)]
-        all_ = pbuf.at[0]
-        this, that = 2 * j + group(j), 2 * j + 1 - group(j)
-        pltpu.make_async_copy(few, few, pr.at[this]).wait()
-        pltpu.make_async_copy(all_, all_, pr.at[that]).wait()
-        handed[:, at(this, LANES)] = pbuf[this]
-        handed[:, at(that, LANES)] = pbuf[that]
-        g_copy(j).wait_recv()
-        gated[:, at(that, LANES)] = grecv[j]
-        g_copy(j).wait_send()
-        for e in (0, 1):
-            pltpu.make_async_copy(some, some, ps.at[j, e]).wait()
-            o_copy(j, e).wait_send()
-            h_copy(j, e).wait_send()
-        for k in range(4):
-            w_pair(j, k).wait_send()
-
-    @pl.loop(0, UNITS)
-    def _(v):
-        w_beside(v).wait_send()
-        w_across(v).wait_send()
-        w_far(v).wait_send()
-
-    @pl.loop(0, MESSAGES)
-    def _(m):
-        for k in (0, 1):
-            t_near(m, k).wait_send()
-            t_next(m, k).wait_send()
-
-    m_copy().wait_send()
-    for sub in range(PARTS):
-        t_x(sub).wait_send()
+    def sent(ref, sem):
+        pltpu.make_async_copy(ref, ref, sem).wait()
+
+    sent(tbuf.at[pl.ds(0, 3)], tys.at[0])
+    sent(wbuf.at[pl.ds(0, 2), pl.ds(0, 6)], ws.at[0])
+    sent(wbuf.at[pl.ds(0, 2)], ws.at[1])
+    sent(osend, os_.at[0])
+    sent(hrecv, hs.at[0])
+    sent(mine, ms)
+    sent(txbuf, txs.at[0])
+    for e in (0, 1):
         for d in (0, 1):
             @pl.when(jnp.logical_not(stays(d)))
             def _():
-                t_z(0, sub, d).wait_send()
-                t_z(1, sub, d).wait_send()
+                sent(txbuf, tzs.at[e, d])
+
+    for e in (0, 1):
+        sent(pbuf.at[e, :, pl.ds(0, 240)], ps.at[e])
+        sent(pbuf.at[e, :, pl.ds(0, 240)], pr.at[e])
+
+    @pl.loop(0, 16)
+    def _(source):
+        rows = at(source, 16)
+        for e in (0, 1):
+            there = (source // 2 + 2 * e) % 4
+            for j in range(CHUNKS):
+                handed[rows, at(2 * j + ((there + j % 2) // 2) % 2, LANES)] = pbuf[e, j, rows]
+
+    for j in range(CHUNKS):
+        g_copy(j).wait_recv()
+        gated[:, at(2 * j + 1 - group(j), LANES)] = grecv[j]
+    sent(gsend, gs.at[0])
 
 
 def per_device(tokens, input_weight, filter_taps, decay_rates, skip_gain, owners):
@@ -413,14 +429,14 @@
             pltpu.VMEM((CHUNKS, 3, HALF, LANES), BF16),
             pltpu.VMEM((4, 2, 2, ROWS, 1024), BF16),
             pltpu.VMEM((ROWS, 1024), BF16),
-            pltpu.VMEM((CHUNKS, ROWS, 3 * LANES), F32),
+            pltpu.VMEM((2, CHUNKS, ROWS, 3 * LANES), F32),
             pltpu.VMEM((CHUNKS, 2, ROWS, 3 * LANES), BF16),
             pltpu.VMEM((CHUNKS, 2, ROWS, 3 * LANES), BF16),
             pltpu.VMEM((CHUNKS, 2, ROWS, LANES), BF16),
             pltpu.VMEM((CHUNKS, 2, ROWS, LANES), BF16),
             pltpu.VMEM((CHUNKS, 2, 128, LANES), BF16),
-            pltpu.VMEM((CHUNKS, 2, ROWS, LANES), BF16),
-            pltpu.VMEM((2 * CHUNKS, ROWS, LANES), BF16),
+            pltpu.VMEM((2, CHUNKS, ROWS, LANES), BF16),
+            pltpu.VMEM((2, CHUNKS, ROWS, LANES), BF16),
             pltpu.VMEM((CHUNKS, ROWS, LANES), BF16),
             pltpu.VMEM((CHUNKS, ROWS, LANES), BF16),
             pltpu.VMEM((32, 128), BF16),
@@ -428,16 +444,24 @@
             pltpu.VMEM((2, ROWS, ROWS), BF16),
             pltpu.VMEM((CHUNKS, 128, LANES), F32),
             pltpu.VMEM((8, 376, LANES), F32),
-            dma((2, CHUNKS)), dma((7, UNITS)), dma((7, UNITS)),
-            dma((PARTS,)), dma((PARTS,)), dma((2, PARTS, 2)), dma((2, 2, PARTS)),
-            dma((4, MESSAGES)), dma((4, MESSAGES)),
-            dma((CHUNKS, 2)), dma((CHUNKS, 2)), dma((CHUNKS, 2)), dma((CHUNKS, 2)),
-            dma((CHUNKS, 2)), dma((2 * CHUNKS,)), dma((CHUNKS,)), dma((CHUNKS,)), dma, dma,
+            dma((2, CHUNKS)), dma((2,)), dma((7, UNITS)),
+            dma((1,)), dma((PARTS,)), dma((2, 2)), dma((2, 2, PARTS)),
+            dma((1,)), dma((4, MESSAGES)),
+            dma((1,)), dma((CHUNKS, 2)), dma((1,)), dma((CHUNKS, 2)),
+            dma((2,)), dma((2,)), dma((1,)), dma((CHUNKS,)), dma, dma,
         ],
         compiler_params=pltpu.CompilerParams(
             collective_id=0, has_side_effects=True, vmem_limit_bytes=56 * 1024 * 1024),
         name="hyena",
     )(tokens, input_weight, filter_taps, decay_rates.reshape(1, -1), skip_gain.reshape(1, -1), owners.reshape(1, -1))
+    def place(a, b, a_out, b_out):
+        a_out[...] = a[...]
+        b_out[...] = b[...]
+
+    gated, handed = pl.pallas_call(
+        place, out_shape=(jax.ShapeDtypeStruct((ROWS, 1024), BF16),) * 2, in_specs=[vmem, vmem], out_specs=(vmem, vmem),
+        name="results",
+    )(gated, handed)
     return gated, handed.reshape(32, 8, 1024)
 
 

time: 137 us -> 117 us (0.85)
  Pallas kernels: 132 us -> 116 us
  local copies, waits for them, and re-layouts: 3.74 us -> 0 us
    pallas_call x1, Pallas kernels: 132 us -> 114 us  [per_device(): pl.pallas_call(kernel, out_shape=(jax.ShapeDtypeStruct((ROWS, 1024), BF16...]
    unnamed x2 -> x0, local copies, waits for them, and re-layouts: 3.74 us -> none
    pallas_call x0 -> x1, Pallas kernels: none -> 2.2 us  [per_device(): pl.pallas_call(place, out_shape=(jax.ShapeDtypeStruct((ROWS, 1024), BF16)...]
where the time goes in v4:
time: 117 us; the launch traced here: 116 us
  Pallas kernels  116 us (99%)
    pallas_call x1, Pallas kernels, per_device(): pl.pallas_call(kernel, out_shape=(jax.ShapeDtypeStruct((ROWS, 1024), BF16...  114 us

profile of v4, /device:TPU:0, one launch (start us, length us, event | category | flops | bytes accessed | tf_op | source)
XLA Modules:
  0.0 116.5 jit_solution(17817355124718818444)
XLA Ops:
  0.6 113.6 %hyena.1 = (bf16[256,1024]{1,0:T(8,128)(2,1)}, bf16[256,1024]{1,0:T(8,128)(2,1)}) custom-call(bf16[256,1024]{1,0:T(8,128)(2,1)} %tok.1, bf16[3,512,1024]{2,1,0:T(8,128)(2,1)} %wgt.1, f32[128,1024]{1,0:T(8,128)} %taps_in.1, f32[1,1024]{1,0:T(1,128)} %bitcast.4, f32[1,1024]{1,0:T(1,128)} %bitcast.5, s32[1,32]{1,0:T(1,128)} %bitcast.6), custom_call_target="tpu_custom_call" | custom-call | tf_op jit(solution)/shard_map/hyena/pallas_call | solution.py:422
  114.3 2.2 %results.1 = (bf16[256,1024]{1,0:T(8,128)(2,1)}, bf16[256,1024]{1,0:T(8,128)(2,1)}) custom-call(bf16[256,1024]{1,0:T(8,128)(2,1)} %get-tuple-element.6.a, bf16[256,1024]{1,0:T(8,128)(2,1)} %get-tuple-element.7.b), custom_call_target="tpu_custom_call" | custom-call | tf_op jit(solution)/shard_map/results/pallas_call | solution.py:461

commit v5 on v4

--- a/solution.py
+++ b/solution.py
@@ -11,12 +11,14 @@
 ROWS, HALF = 256, 512
 PARTS = 4
 SUB, MESSAGES = ROWS // PARTS, 4 * PARTS
-AHEAD, UNITS, W_AHEAD, W_LEAD = 4, 3 * CHUNKS, 3, 1
+ORDER = [(m + PARTS // 2) % PARTS for m in range(PARTS)]
+HALF_ROWS = ROWS // 2
+AHEAD, UNITS, W_AHEAD, W_LEAD = 5, 3 * CHUNKS, 3, 1
 
 
 def kernel(tok, wgt, taps_in, decay, skip, owners, gated, handed,
            wbuf, wother, tbuf, txbuf, own, osend, orecv, qbuf, ubuf, hrecv, psend, pbuf, gsend, grecv,
-           mine, theirs, sel, taps, shifts,
+           mine, theirs, sel, taps, shifts, prior,
            wl, ws, wr, txs, txr, tzs, tzr, tys, tyr, os_, or_, hs, hr, ps, pr, gs, gr, ms, mr):
     s, c = lax.axis_index("seq"), lax.axis_index("chan")
     core, x, zh = s % 2, (s // 2) % 4, s // 8
@@ -143,9 +145,12 @@
         r = m // PARTS
         return jnp.where(r < 2, zo, zh), jnp.where(r < 2, r, (early + r) % 2)
 
+    def part_of(m):
+        return (m + PARTS // 2) % PARTS
+
     def t_piece(yy, m):
         z, e = block_of(m)
-        return tbuf.at[yy, z, e, at(m % PARTS, SUB)]
+        return tbuf.at[yy, z, e, at(part_of(m), SUB)]
 
     def t_near(m, k):
         piece = t_piece(y, m)
@@ -153,19 +158,18 @@
 
     def t_next(m, k):
         z, e = block_of(m)
-        piece = tbuf.at[(y + 3 - 2 * k) % 4, z, e, at((m % PARTS) * 2 + k, SUB // 2)]
+        piece = tbuf.at[(y + 3 - 2 * k) % 4, z, e, at(part_of(m) * 2 + k, SUB // 2)]
         return remote(piece, piece, tys.at[0], tyr.at[2 + k, m], dev(zh, x, core, zl, (y + 1 + 2 * k) % 4))
 
     def t_along_y(m):
         z, e = block_of(m)
         piece = t_piece(y, m)
-        pltpu.make_async_copy(piece, piece, tzr.at[z, e, m % PARTS]).wait()
+        pltpu.make_async_copy(piece, piece, tzr.at[z, e, part_of(m)]).wait()
         t_near(m, 0).start()
         t_near(m, 1).start()
 
-    for sub in range(PARTS):
+    for sub in ORDER:
         t_x(sub).start()
-    for sub in range(PARTS):
         t_along_z(0, sub)
     for v in range(W_AHEAD):
         w_send(v)
@@ -186,13 +190,13 @@
     t_along_y(0)
     t_along_y(1)
     w_step(0)
-    for sub in range(PARTS):
+    for step, sub in enumerate(ORDER):
         t_x(sub).wait_recv()
         t_along_z(1, sub)
-        if sub + 2 < AHEAD:
-            t_along_y(sub + 2)
-        if sub + 1 < W_LEAD:
-            w_step(sub + 1)
+        if step + 2 < AHEAD:
+            t_along_y(step + 2)
+        if step + 1 < W_LEAD:
+            w_step(step + 1)
 
     def order(place):
         spread = (iota((ROWS, 32), 0) // 8 == iota((ROWS, 32), 1)).astype(BF16)
@@ -242,96 +246,135 @@
         source = (zh * 4 + (x + 2 * e) % 4) * 2 + core
         pbuf[e, :, at(source, 16)] = psend[e, :, at(s, 16)]
 
-    def g_copy(j):
-        return remote(gsend.at[j], grecv.at[j], gs.at[0], gr.at[j], dev(zh, x2, core, zl, y))
+    def g_copy(j, rows):
+        return remote(gsend.at[j, rows], grecv.at[j, rows], gs.at[0], gr.at[0], dev(zh, x2, core, zl, y))
+
+    def matmul_pair(pair, z, e, rows):
+        t = jnp.concatenate([tbuf[yy, z, e, rows] for yy in range(4)], axis=1)
+        w = jnp.concatenate([jnp.concatenate([wbuf[2 * pair + q, k, p] for k in range(8)], axis=0)
+                             for q in (0, 1) for p in range(3)], axis=1)
+        both = jnp.dot(t, w, preferred_element_type=F32)
+        return both[:, :3 * LANES], both[:, 3 * LANES:]
 
     def stage_other(n):
-        e = jnp.where(n < 2, 0, jnp.where(n < 4, 1, n % 2))
-        j = jnp.where(n < 2, n, jnp.where(n < 4, n - 2, n // 2))
+        e = jnp.where(n < 2, 0, jnp.where(n % 2 == 0, early, 1 - early))
+        j = jnp.where(n < 2, n, n // 2 + 1)
         osend[j, e] = matmul(j, zo, e).astype(BF16)
         o_copy(j, e).start()
+
+    def stage_other_half(half):
+        rows = at(half, HALF_ROWS)
+        for j, part in enumerate(matmul_pair(0, zo, 1, rows)):
+            osend[j, 1, rows] = part.astype(BF16)
+            remote(osend.at[j, 1, rows], orecv.at[j, 1, rows], os_.at[0], or_.at[j, 1], dev(zo, x, core, zl, y)).start()
 
     def stage_own(n):
         late = n // 4
         pair = jnp.where(n < 4, n // 2, n % 2)
-        rows = at(jnp.where(n < 4, n % 2, (n - 4) // 2), ROWS // 2)
+        rows = at(jnp.where(n < 4, n % 2, 1 - (n - 4) // 2), HALF_ROWS)
         e = jnp.where(n < 4, early, 1 - early)
-        t = jnp.concatenate([tbuf[yy, zh, e, rows] for yy in range(4)], axis=1)
-        w = jnp.concatenate([jnp.concatenate([wbuf[2 * pair + q, k, p] for k in range(8)], axis=0)
-                             for q in (0, 1) for p in range(3)], axis=1)
-        both = jnp.dot(t, w, preferred_element_type=F32)
-        for q in (0, 1):
-            own[late, 2 * pair + q, rows] = both[:, 3 * LANES * q:3 * LANES * (q + 1)]
-
-    def stage_u(j, e, late):
-        o_copy(j, e).wait_recv()
-        full = (own[late, j] + orecv[j, e].astype(F32)).astype(BF16)
-        qbuf[j, e] = full[:, :LANES]
-        u = (full[:, LANES:2 * LANES].astype(F32) * full[:, 2 * LANES:].astype(F32)).astype(BF16)
-        ubuf[j, e] = u
-        h_copy(j, e).start()
-        psend[e, j] = jnp.dot(sel[e], u, preferred_element_type=F32).astype(BF16)
-
-        @pl.when(j == CHUNKS - 1)
-        def _():
+        for q, part in enumerate(matmul_pair(pair, zh, e, rows)):
+            own[late, 2 * pair + q, rows] = part
+
+    def stage_u(n):
+        late = n // 8
+        j = jnp.where(n < 8, n // 2, n % 4)
+        half = 1 - jnp.where(n < 8, n % 2, (n - 8) // 4)
+        e, rows = jnp.where(n < 8, early, 1 - early), at(half, HALF_ROWS)
+
+        @pl.when(half == 1)
+        def _():
+            o_copy(j, e).wait_recv()
+
+        full = (own[late, j, rows] + orecv[j, e, rows].astype(F32)).astype(BF16)
+        qbuf[j, e, rows] = full[:, :LANES]
+        ubuf[j, e, rows] = (full[:, LANES:2 * LANES].astype(F32) * full[:, 2 * LANES:].astype(F32)).astype(BF16)
+
+        @pl.when(half == 1)
+        def _():
+            h_copy(j, e).start()
+
+        @pl.when((n == 7) | (n == 15))
+        def _():
+            @pl.loop(0, CHUNKS)
+            def _(jj):
+                psend[e, jj] = jnp.dot(sel[e], ubuf[jj, e], preferred_element_type=F32).astype(BF16)
+
             stage_pages(e)
 
-    def stage_filter(j, e):
+    def wait_prior(j, e):
         pltpu.make_async_copy(hrecv.at[j, e], hrecv.at[j, e], hr.at[j, e]).wait()
         first = (zh == 0) & (core == 0) & ((x + 2 * e) % 4 == 0)
-        prior = jnp.where(first, 0.0, hrecv[j, e].astype(F32))
-        ext = jnp.concatenate([prior, ubuf[j, e].astype(F32)], axis=0)
+        return jnp.where(first, 0.0, hrecv[j, e].astype(F32))
+
+    def filtered(j, before, u):
+        count = u.shape[0] // 16
+        ext = jnp.concatenate([before, u.astype(F32)], axis=0)
         for b in range(8):
-            shifts[b] = ext[8 - b:384 - b]
-
-        def stream(count, tap, data):
-            def add(b, sums):
-                x_ = [data(b, m) for m in range(count + 7)]
-                sums = list(sums)
+            shifts[b, :ext.shape[0] - 8] = ext[8 - b:ext.shape[0] - b]
+
+        def stream(groups, tap, data):
+            sums = [jnp.zeros((8, LANES), F32) for _ in range(groups)]
+            for b in range(8):
+                x_ = [data(b, m) for m in range(groups + 7)]
                 for a in range(8):
                     weight = jnp.broadcast_to(tap(b, a), (8, LANES))
-                    for r in range(count):
+                    for r in range(groups):
                         sums[r] = sums[r] + weight * x_[r - a + 7]
-                return tuple(sums)
-            return lax.fori_loop(0, 8, add, tuple(jnp.zeros((8, LANES), F32) for _ in range(count)), unroll=2)
+            return sums
 
         def rows_of(b, m):
             return shifts[b, 8 * m:8 * m + 8]
 
         def tap_of(b, a):
-            return taps[j, pl.ds(8 * a + b, 1)]
-
-        even = stream(16, lambda b, a: tap_of(b, 2 * a), lambda b, m: rows_of(b, 2 * m + 1))
-        odd = stream(17, lambda b, a: tap_of(b, 2 * a + 1), lambda b, m: rows_of(b, 2 * m))
-        both = stream(16, lambda b, a: tap_of(b, 2 * a) + tap_of(b, 2 * a + 1),
+            return taps[j, 8 * a + b:8 * a + b + 1]
+
+        even = stream(count, lambda b, a: tap_of(b, 2 * a), lambda b, m: rows_of(b, 2 * m + 1))
+        odd = stream(count + 1, lambda b, a: tap_of(b, 2 * a + 1), lambda b, m: rows_of(b, 2 * m))
+        both = stream(count, lambda b, a: tap_of(b, 2 * a) + tap_of(b, 2 * a + 1),
                       lambda b, m: rows_of(b, 2 * m + 1) + rows_of(b, 2 * m + 2))
-        z = jnp.concatenate(
-            [piece for r in range(16) for piece in (even[r] + odd[r], both[r] - even[r] - odd[r + 1])], axis=0)
-        out = (qbuf[j, e].astype(F32) * z).astype(BF16)
+        return jnp.concatenate(
+            [piece for r in range(count) for piece in (even[r] + odd[r], both[r] - even[r] - odd[r + 1])], axis=0)
+
+    def finish(j, e, rows, z):
+        out = (qbuf[j, e, rows].astype(F32) * z).astype(BF16)
 
         @pl.when(e == 1)
         def _():
-            gsend[j] = out
-            g_copy(j).start()
+            gsend[j, rows] = out
+            g_copy(j, rows).start()
 
         @pl.when(e == 0)
         def _():
-            gated[:, at(2 * j + group(j), LANES)] = out
-
-    waits = (zh == 1) & (core == 0) & (x % 2 == 0)
-    now = jnp.where(waits, 0, 3)
+            gated[rows, at(2 * j + group(j), LANES)] = out
+
+    def stage_filter(j, half):
+        @pl.when(half == 0)
+        def _():
+            prior[...] = wait_prior(j, early)
+
+        @pl.when(half == 1)
+        def _():
+            prior[...] = ubuf[j, early, :HALF_ROWS].astype(F32)
+
+        rows = at(half, HALF_ROWS)
+        finish(j, early, rows, filtered(j, prior[...], ubuf[j, early, rows]))
+
+    def stage_filter_whole(j):
+        e = 1 - early
+        finish(j, e, pl.ds(0, ROWS), filtered(j, wait_prior(j, e), ubuf[j, e]))
 
     def others_done(i):
-        return jnp.where(i < 4, 0, jnp.where(i < 8, i // 2 - 1, jnp.where(i < 11, i - 4, jnp.where(i < 12, 6, 8))))
+        return jnp.where(i < 4, 0, jnp.where(i < 9, jnp.minimum(i // 2 - 1, 2), jnp.where(i < 12, 4, 6)))
 
     def owns_done(i):
         return jnp.where(i < 13, 0, jnp.where(i < 16, 2 * (i - 12), 6))
 
     def us_done(i):
-        return jnp.where(i < 13, 0, jnp.where(i == 13, 2, jnp.where(i < 16, 3, 8)))
+        return jnp.where(i < 13, 0, jnp.where(i == 13, 4, jnp.where(i == 14, 6, jnp.where(i == 15, 12, 16))))
 
     def filters_done(i):
-        return jnp.where(i < 16, 0, 8)
+        return jnp.where(i < 14, 0, jnp.where(i == 14, 2, jnp.where(i == 15, 4, 12)))
 
     @pl.loop(0, MESSAGES + 1)
     def _(i):
@@ -364,23 +407,33 @@
         def _(n):
             stage_other(n)
 
+        @pl.when((i == 6) | (i == 8))
+        def _():
+            stage_other_half((8 - i) // 2)
+
         @pl.loop(owns_done(i - 1), owns_done(i))
         def _(n):
             stage_own(n)
 
         @pl.loop(us_done(i - 1), us_done(i))
         def _(n):
-            late = n // CHUNKS
-
-            @pl.when((late == 1) & (n % 2 == 0))
-            def _():
-                stage_own(6 + n % CHUNKS // 2)
-
-            stage_u(n % CHUNKS, jnp.where(late == 1, 1 - early, early), late)
+            @pl.when((n == 12) | (n == 14))
+            def _():
+                stage_own(n // 2)
+
+            stage_u(n)
 
         @pl.loop(filters_done(i - 1), filters_done(i))
         def _(n):
-            stage_filter(n % CHUNKS, jnp.where(n < CHUNKS, early, 1 - early))
+            sooner = (n < 4) | ((n // 4 + early) % 2 == 0)
+
+            @pl.when(sooner)
+            def _():
+                stage_filter(n % 4, jnp.where(n < 4, 1, 0))
+
+            @pl.when(jnp.logical_not(sooner))
+            def _():
+                stage_filter_whole(n % 4)
 
     def sent(ref, sem):
         pltpu.make_async_copy(ref, ref, sem).wait()
@@ -410,8 +463,8 @@
             for j in range(CHUNKS):
                 handed[rows, at(2 * j + ((there + j % 2) // 2) % 2, LANES)] = pbuf[e, j, rows]
 
+    sent(gsend, gr.at[0])
     for j in range(CHUNKS):
-        g_copy(j).wait_recv()
         gated[:, at(2 * j + 1 - group(j), LANES)] = grecv[j]
     sent(gsend, gs.at[0])
 
@@ -443,12 +496,13 @@
             pltpu.VMEM((32, 128), BF16),
             pltpu.VMEM((2, ROWS, ROWS), BF16),
             pltpu.VMEM((CHUNKS, 128, LANES), F32),
-            pltpu.VMEM((8, 376, LANES), F32),
+            pltpu.VMEM((8, ROWS + 120, LANES), F32),
+            pltpu.VMEM((HALF_ROWS, LANES), F32),
             dma((2, CHUNKS)), dma((2,)), dma((7, UNITS)),
             dma((1,)), dma((PARTS,)), dma((2, 2)), dma((2, 2, PARTS)),
             dma((1,)), dma((4, MESSAGES)),
             dma((1,)), dma((CHUNKS, 2)), dma((1,)), dma((CHUNKS, 2)),
-            dma((2,)), dma((2,)), dma((1,)), dma((CHUNKS,)), dma, dma,
+            dma((2,)), dma((2,)), dma((1,)), dma((1,)), dma, dma,
         ],
         compiler_params=pltpu.CompilerParams(
             collective_id=0, has_side_effects=True, vmem_limit_bytes=56 * 1024 * 1024),

time: 117 us -> 115 us (0.983)
  Pallas kernels: 116 us -> 113 us
    pallas_call x1, Pallas kernels: 114 us -> 111 us  [per_device(): pl.pallas_call(kernel, out_shape=(jax.ShapeDtypeStruct((ROWS, 1024), BF16...]
where the time goes in v5:
time: 115 us; the launch traced here: 114 us
  Pallas kernels  113 us (98%)
    pallas_call x1, Pallas kernels, per_device(): pl.pallas_call(kernel, out_shape=(jax.ShapeDtypeStruct((ROWS, 1024), BF16...  111 us

profile of v5, /device:TPU:0, one launch (start us, length us, event | category | flops | bytes accessed | tf_op | source)
XLA Modules:
  0.0 114.0 jit_solution(13202693275136995838)
XLA Ops:
  0.6 111.1 %hyena.1 = (bf16[256,1024]{1,0:T(8,128)(2,1)}, bf16[256,1024]{1,0:T(8,128)(2,1)}) custom-call(bf16[256,1024]{1,0:T(8,128)(2,1)} %tok.1, bf16[3,512,1024]{2,1,0:T(8,128)(2,1)} %wgt.1, f32[128,1024]{1,0:T(8,128)} %taps_in.1, f32[1,1024]{1,0:T(1,128)} %bitcast.4, f32[1,1024]{1,0:T(1,128)} %bitcast.5, s32[1,32]{1,0:T(1,128)} %bitcast.6), custom_call_target="tpu_custom_call" | custom-call | tf_op jit(solution)/shard_map/hyena/pallas_call | solution.py:475
  111.8 2.2 %results.1 = (bf16[256,1024]{1,0:T(8,128)(2,1)}, bf16[256,1024]{1,0:T(8,128)(2,1)}) custom-call(bf16[256,1024]{1,0:T(8,128)(2,1)} %get-tuple-element.6.a, bf16[256,1024]{1,0:T(8,128)(2,1)} %get-tuple-element.7.b), custom_call_target="tpu_custom_call" | custom-call | tf_op jit(solution)/shard_map/results/pallas_call | solution.py:515

commit v6 on v5

--- a/solution.py
+++ b/solution.py
@@ -374,7 +374,7 @@
         return jnp.where(i < 13, 0, jnp.where(i == 13, 4, jnp.where(i == 14, 6, jnp.where(i == 15, 12, 16))))
 
     def filters_done(i):
-        return jnp.where(i < 14, 0, jnp.where(i == 14, 2, jnp.where(i == 15, 4, 12)))
+        return jnp.where(i < 13, 0, jnp.where(i == 13, 1, jnp.where(i == 14, 3, jnp.where(i == 15, 4, 12))))
 
     @pl.loop(0, MESSAGES + 1)
     def _(i):

time: 115 us -> 115 us (level)
  no operation moved by 1% of the time
where the time goes in v6:
time: 115 us
  Pallas kernels  114 us (99%)
    pallas_call x1, Pallas kernels, per_device(): pl.pallas_call(kernel, out_shape=(jax.ShapeDtypeStruct((ROWS, 1024), BF16...  112 us

profile of v6, /device:TPU:0, one launch (start us, length us, event | category | flops | bytes accessed | tf_op | source)
XLA Modules:
  0.0 114.5 jit_solution(2522541544425091264)
XLA Ops:
  0.6 111.7 %hyena.1 = (bf16[256,1024]{1,0:T(8,128)(2,1)}, bf16[256,1024]{1,0:T(8,128)(2,1)}) custom-call(bf16[256,1024]{1,0:T(8,128)(2,1)} %tok.1, bf16[3,512,1024]{2,1,0:T(8,128)(2,1)} %wgt.1, f32[128,1024]{1,0:T(8,128)} %taps_in.1, f32[1,1024]{1,0:T(1,128)} %bitcast.4, f32[1,1024]{1,0:T(1,128)} %bitcast.5, s32[1,32]{1,0:T(1,128)} %bitcast.6), custom_call_target="tpu_custom_call" | custom-call | tf_op jit(solution)/shard_map/hyena/pallas_call | solution.py:475
  112.3 2.2 %results.1 = (bf16[256,1024]{1,0:T(8,128)(2,1)}, bf16[256,1024]{1,0:T(8,128)(2,1)}) custom-call(bf16[256,1024]{1,0:T(8,128)(2,1)} %get-tuple-element.6.a, bf16[256,1024]{1,0:T(8,128)(2,1)} %get-tuple-element.7.b), custom_call_target="tpu_custom_call" | custom-call | tf_op jit(solution)/shard_map/results/pallas_call | solution.py:515
